TPU v7x, 32 devices: a whole 2x2x4 slice. The times are simulated.
32 devices in a mesh: mem: 4 (over y, x), lat: 8 (over z, core).
Axes of the slice: x: 2, y: 2, z: 4, core: 2. Of those that a mesh axis runs over, the one named last changes fastest.
Arguments:
- prior_member_stack: float32 [64, 16, 64, 512], P('mem', None, 'lat'), may hold values from -6 to 6
- zonal_stability_ratio: float32 [64, 512], P('lat'), may hold values from -0.45 to 0.45
- meridional_stability_ratio: float32 [64, 512], P('lat'), may hold values from -0.45 to 0.45
- obs_perturb: bfloat16 [512, 64, 4096], P(('mem', 'lat')), may hold values from -2 to 2
- innovation: float32 [512, 4096], P(('mem', 'lat')), may hold values from -6 to 6
- inverse_error_variance: float32 [512, 4096], P(('mem', 'lat')), may hold values from 0.25 to 4
- obs_count: int32 [512], P(('mem', 'lat')), may hold values from 1 to 4096, 1048576 in all
- neighbours: int32 [512, 6], P(('mem', 'lat')), may hold values from 0 to 47, as said below
- localization: float32 [512, 6], P(('mem', 'lat')), may hold values from 0.2 to 1
Outputs:
- analysis: float32 [64, 16, 512, 64], P(None, None, ('mem', 'lat'))
Inputs may be any that keep to these rules, and one draw needn't show every extreme that they name: The observations of a tile fill its first obs_count slots; later slots are ignored. `neighbours`: window index w names row group w % 16 of the strip w // 16 - 1 places east (strips wrap around). Entry 0 of each row is the tile itself; the others are distinct tiles of the previous, same or next row group in the previous, same or next strip.
All inputs are finite; a program needn't handle non-finite values. No bound on the sum of `obs_count` on one device may be relied on, other than what follows from the above.
Results may differ from a plain program's by a relative error of at most 0.0022.
Values may be sent and summed in bfloat16 or wider, within the bound.
A program may use at most 256 MiB of HBM per device.

v0:
```python
import jax
import jax.numpy as jnp
from jax import lax
from jax.sharding import PartitionSpec as P

NS_ITERS = 5


def extended(x, sides, width, wrap):
    for axis, dim in sides:
        size, length = (lax.axis_size(axis), x.shape[dim])
        up = [(i, (i + 1) % size) for i in range(size if wrap else size - 1)]
        down = [(j, i) for i, j in up]
        last = lax.slice_in_dim(x, length - width, length, axis=dim)
        leading = lax.slice_in_dim(x, 0, width, axis=dim)
        before = lax.ppermute(last, axis, up)
        after = lax.ppermute(leading, axis, down)
        x = jnp.concatenate([before, x, after], axis=dim)
    return x


def tile_terms(perturb, weight, drive):
    weighted = (perturb.astype(jnp.float32) * weight.astype(jnp.float32)[:, None, :]).astype(
        jnp.bfloat16
    )
    gram_matrix = jnp.einsum("tko,tlo->tkl", weighted, perturb, preferred_element_type=jnp.float32)
    drive_vector = jnp.einsum("tko,to->tk", perturb, drive, preferred_element_type=jnp.float32)
    return (gram_matrix, drive_vector)


def transform_weights(curvature, drive_total, members):
    frob_scale = jnp.sqrt(jnp.sum(curvature * curvature, axis=(1, 2)))
    identity = jnp.eye(members, dtype=jnp.float32)[None]
    current = curvature / frob_scale[:, None, None]
    inverse = jnp.broadcast_to(identity, curvature.shape)
    for _ in range(NS_ITERS):
        middle = 1.5 * identity - 0.5 * jnp.einsum(
            "tij,tjk->tik", inverse, current, precision=lax.Precision.HIGHEST
        )
        current = jnp.einsum("tij,tjk->tik", current, middle, precision=lax.Precision.HIGHEST)
        inverse = jnp.einsum("tij,tjk->tik", middle, inverse, precision=lax.Precision.HIGHEST)
    spread_part = jnp.sqrt((members - 1.0) / frob_scale)[:, None, None] * inverse
    half_step = jnp.einsum("tij,tj->ti", inverse, drive_total, precision=lax.Precision.HIGHEST)
    ensemble_mean_portion = (
        jnp.einsum("tij,tj->ti", inverse, half_step, precision=lax.Precision.HIGHEST)
        / frob_scale[:, None]
    )
    return spread_part + ensemble_mean_portion[:, :, None]


def per_device(
    prior_member_stack,
    zonal_stability_ratio,
    meridional_stability_ratio,
    obs_perturb,
    innovation,
    inverse_error_variance,
    obs_count,
    neighbours,
    localization,
):
    members_dev, channels, row_count, lon_count = prior_member_stack.shape
    mem_count = lax.axis_size("mem")
    lat_count = lax.axis_size("lat")
    lon_strip = lon_count // (mem_count * lat_count)
    members = members_dev * mem_count
    lat_total = row_count * lat_count
    east_neighbour = jnp.roll(prior_member_stack, -1, axis=-1)
    eastward_flux = (
        jnp.maximum(zonal_stability_ratio, 0.0) * prior_member_stack
        + jnp.minimum(zonal_stability_ratio, 0.0) * east_neighbour
    )
    divergence_x = eastward_flux - jnp.roll(eastward_flux, 1, axis=-1)
    stacked = jnp.concatenate(
        [
            prior_member_stack.reshape(members_dev * channels, row_count, lon_count),
            meridional_stability_ratio[None],
        ],
        axis=0,
    )
    padded = extended(stacked, (("lat", 1),), 1, False)
    fields_ext = padded[:-1].reshape(members_dev, channels, row_count + 2, lon_count)
    north_ext = padded[-1, :-1]
    flux_north = (
        jnp.maximum(north_ext, 0.0) * fields_ext[:, :, : row_count + 1]
        + jnp.minimum(north_ext, 0.0) * fields_ext[:, :, 1:]
    )
    transported_quantities = (
        prior_member_stack - divergence_x - (flux_north[:, :, 1:] - flux_north[:, :, :-1])
    )
    rows_last = jnp.swapaxes(transported_quantities, 2, 3)
    moved = rows_last.reshape(1, members_dev, channels, lon_count, row_count)
    arrived = lax.all_to_all(moved, ("mem", "lat"), split_axis=3, concat_axis=0, tiled=True)
    arrived = arrived.reshape(mem_count, lat_count, members_dev, channels, lon_strip, row_count)
    arrived = jnp.transpose(arrived, (0, 2, 3, 4, 1, 5)).reshape(
        members, channels, lon_strip, lat_total
    )
    blocks_per_processor, obs_cap = innovation.shape
    neigh_count = neighbours.shape[1]
    window_tiles = 3 * blocks_per_processor
    is_valid = (
        lax.broadcasted_iota(jnp.int32, (blocks_per_processor, obs_cap), 1) < obs_count[:, None]
    )
    obs_weight = jnp.where(is_valid, inverse_error_variance, 0.0).astype(jnp.bfloat16)
    obs_drive = jnp.where(is_valid, inverse_error_variance * innovation, 0.0).astype(jnp.bfloat16)
    window_slots = lax.broadcasted_iota(jnp.int32, (blocks_per_processor, window_tiles), 1)
    combine = jnp.zeros((blocks_per_processor, window_tiles), jnp.float32)
    for slot_index in range(neigh_count):
        combine = combine + jnp.where(
            neighbours[:, slot_index, None] == window_slots, localization[:, slot_index, None], 0.0
        )
    observed = jnp.concatenate([obs_perturb, obs_weight[:, None, :], obs_drive[:, None, :]], axis=1)
    received = extended(observed, ((("mem", "lat"), 0),), blocks_per_processor, True)
    gram_matrix, drive_vector = tile_terms(
        received[:, :members], received[:, members], received[:, members + 1]
    )
    window = jnp.concatenate([gram_matrix, drive_vector[:, None, :]], axis=1)
    gathered = jnp.einsum("ts,skl->tkl", combine, window, precision=lax.Precision.HIGHEST)
    curvature = (members - 1.0) * jnp.eye(members, dtype=jnp.float32)[None] + gathered[:, :members]
    drive_total = gathered[:, members]
    weights = transform_weights(curvature, drive_total, members)
    grid = arrived.reshape(
        members, channels, lon_strip, blocks_per_processor, lat_total // blocks_per_processor
    )
    member_mean = jnp.mean(grid, axis=0)
    anomaly = grid - member_mean
    update = jnp.einsum("icxtr,tij->jcxtr", anomaly, weights, precision=lax.Precision.HIGHEST)
    return (member_mean + update).reshape(members, channels, lon_strip, lat_total)


def solution(mesh):
    in_specs = (
        P("mem", None, "lat", None),
        P("lat", None),
        P("lat", None),
        P(("mem", "lat"), None, None),
        P(("mem", "lat"), None),
        P(("mem", "lat"), None),
        P(("mem", "lat")),
        P(("mem", "lat"), None),
        P(("mem", "lat"), None),
    )
    out_specs = P(None, None, ("mem", "lat"), None)
    return jax.shard_map(
        per_device, mesh=mesh, in_specs=in_specs, out_specs=out_specs, check_vma=False
    )
```

profile of v0, /device:TPU:0, one launch (start us, length us, event | category | flops | bytes accessed | tf_op | source)
XLA Modules:
  0.0 553.9 jit_solution(14655659342310174099)
XLA Ops:
  2.7 8.1 %pad_maximum_fusion.1 = bf16[16,66,4096]{2,1,0:T(8,128)(2,1)} fusion(bf16[16,1,4096]{2,1,0:T(2,128)(2,1)S(1)} %copy.193, bf16[16,1,4096]{2,1,0:T(2,128)(2,1)S(1)} %copy.192, bf16[16,64,4096]{2,1,0:T(8,128)(2,1)} %param.12), kind=kLoop, calls=%fused_computation.7 | loop fusion | flops 25952256 | bytes 17301504 | tf_op jit(solution)/shard_map/concatenate | solution.py:112
  10.8 11.7 %copy.194 = bf16[16,66,4096]{2,0,1:T(8,128)(2,1)} copy(bf16[16,66,4096]{2,1,0:T(8,128)(2,1)} %pad_maximum_fusion.1) | data formatting | bytes 17301504 | tf_op jit(solution)/shard_map/concatenate | solution.py:112
  22.5 6.4 %collective-permute-start.3 = (bf16[16,66,4096]{2,0,1:T(8,128)(2,1)}, bf16[16,66,4096]{2,0,1:T(8,128)(2,1)}, u32[]{:S(2)}, u32[]{:S(2)}) collective-permute-start(bf16[16,66,4096]{2,0,1:T(8,128)(2,1)} %copy.194), channel_id=1, source_target_pairs={{1,0},{2,1},{3,2},{4,3},{5,4},{6,5},{7,6},{8,7},{9,8},{10,9},{11,1... | collective-permute-start | bytes 25952264 | tf_op jit(solution)/shard_map/ppermute | solution.py:17
  28.9 3.9 fusion.27
  32.8 2.1 collective-permute-start
  34.9 1.5 collective-permute-start.1
  36.4 1.3 slice.93
  37.7 3.2 slice.92
  42.3 3.1 pad_maximum_fusion.5
  45.7 4.7 fusion.10
  51.2 2.4 copy.183
  56.8 8.5 %fusion.8 = f32[1,16,16,512,8]{3,2,1,4,0:T(8,128)} fusion(f32[16,16,9,512]{3,1,0,2:T(8,128)S(1)} %fusion.6, f32[16,16,8,512]{3,1,0,2:T(8,128)S(1)} %fusion.10, f32[16,16,8,511]{3,1,0,2:T(8,128)S(1)} %bitcast.119, f32[16,16,8,1]{3,1,0,2:T(8,128)S(1)} %slice.121, f32[16,16,8,512]{3,2,1,0:T(8,128)S(1)} %copy-done.1), kind=kLoop, calls=%fused_computation.21 | loop fusion | flops 5242880 | bytes 25165824 | tf_op jit(solution)/shard_map/reshape | solution.py:92
  65.3 26.4 %copy.187 = f32[1,16,16,512,8]{2,4,1,0,3:T(8,128)} copy(f32[1,16,16,512,8]{3,2,1,4,0:T(8,128)} %fusion.8) | data formatting | bytes 8388608 | tf_op jit(solution)/shard_map/reshape | solution.py:92
  91.8 29.0 %reshape.89 = f32[32,1,32768]{2,1,0:T(1,128)} reshape(f32[512,1,16,8,16]{4,3,2,1,0:T(8,128)} %bitcast.115) | data formatting | bytes 8388608
  120.8 170.5 %all-to-all-start = ((f32[32,1,32768]{2,1,0:T(1,128)}), f32[32,1,32768]{2,1,0:T(1,128)}, u32[]{:S(2)}, u32[]{:S(2)}) async-start(f32[32,1,32768]{2,1,0:T(1,128)} %reshape.89), calls=%async_computation | async-start | bytes 8388608 | tf_op jit(solution)/shard_map/all_to_all | solution.py:93
  291.3 11.9 %copy.197 = bf16[16,66,4096]{2,1,0:T(8,128)(2,1)} copy(bf16[16,66,4096]{2,0,1:T(8,128)(2,1)} %collective-permute-done.3) | data formatting | bytes 17301504 | tf_op jit(solution)/shard_map/ppermute | solution.py:17
  303.2 11.9 %copy.196 = bf16[16,66,4096]{2,1,0:T(8,128)(2,1)} copy(bf16[16,66,4096]{2,0,1:T(8,128)(2,1)} %collective-permute-done.2) | data formatting | bytes 17301504 | tf_op jit(solution)/shard_map/ppermute | solution.py:16
  315.1 2.3 maximum_convert_fusion
  317.5 19.7 %pad_maximum_fusion = bf16[48,66,4096]{2,1,0:T(8,128)(2,1)} fusion(bf16[16,66,4096]{2,1,0:T(8,128)(2,1)} %copy.197, bf16[16,1,4096]{2,1,0:T(2,128)(2,1)S(1)} %copy.193, bf16[16,1,4096]{2,1,0:T(2,128)(2,1)S(1)} %copy.192, bf16[16,64,4096]{2,1,0:T(8,128)(2,1)} %param.12, bf16[16,66,4096]{2,1,0:T(8,128)(2,1)} %copy.196), kind=kLoop, calls=%fused_computation.2 | loop fusion | flops 129761280 | bytes 51904512 | tf_op jit(solution)/shard_map/concatenate | solution.py:18
  337.7 17.6 %fusion = f32[48,64,64]{1,2,0:T(8,128)S(1)} fusion(f32[48,4096]{1,0:T(8,128)S(1)} %bitcast.123, bf16[48,66,4096]{2,1,0:T(8,128)(2,1)} %pad_maximum_fusion), kind=kOutput, calls=%fused_computation.1 | convolution fusion | flops 1648361472 | bytes 51904512 | tf_op jit(solution)/shard_map/tko,tlo->tkl/dot_general | solution.py:26
  355.3 13.1 %fusion.3 = f32[48,1,64]{1,2,0:T(8,128)} fusion(bf16[48,66,4096]{2,1,0:T(8,128)(2,1)} %pad_maximum_fusion, bf16[16,66,4096]{2,1,0:T(8,128)(2,1)} %copy.197, bf16[16,66,4096]{2,1,0:T(8,128)(2,1)} %copy.196, bf16[16,1,4096]{2,1,0:T(2,128)(2,1)S(1)} %copy.193, bf16[16,1,4096]{2,1,0:T(2,128)(2,1)S(1)} %copy.192, bf16[16,64,4096]{2,1,0:T(8,128)(2,1)} %param.12), kind=kOutput, calls=%fused_computation.5 | convolution fusion | flops 27131904 | bytes 52703232 | tf_op jit(solution)/shard_map/broadcast_in_dim | solution.py:117
  368.4 1.9 pad_maximum_fusion.6
  370.3 1.7 fusion.12
  384.3 2.1 all-to-all-done
  386.9 13.8 %reduce.1 = f32[32,32768]{1,0:T(8,128)} reduce(f32[32,1,32768]{2,1,0:T(1,128)} %all-to-all-done, f32[]{:T(128)} %broadcast.80), dimensions={1}, to_apply=%all_to_all.11.reduce_sub_computation | reduce | bytes 8388612 | tf_op jit(solution)/shard_map/all_to_all | solution.py:93
  400.6 28.9 %reshape.90 = f32[512,1,16,8,16]{4,3,2,1,0:T(8,128)} reshape(f32[32,32768]{1,0:T(8,128)} %reduce.1) | data formatting | bytes 8388608
  429.5 41.9 %copy.189 = f32[4,8,16,16,16,8]{2,0,4,5,1,3:T(4,128)} copy(f32[4,8,16,16,16,8]{3,5,2,4,1,0:T(8,128)} %bitcast.116) | data formatting | bytes 8388608 | tf_op jit(solution)/shard_map/reshape | solution.py:94
  471.4 29.4 %bitcast_reduce_fusion = f32[16,16,8,8]{1,3,2,0:T(8,128)S(1)} fusion(f32[4,8,16,16,16,8]{2,0,4,5,1,3:T(4,128)} %copy.189), kind=kLoop, calls=%fused_computation.131 | loop fusion | flops 1032192 | bytes 4259840 | tf_op jit(solution)/shard_map/reduce_sum | solution.py:125
  500.9 25.7 %reshape_reshape.3 = f32[64,16,16,16,4]{0,2,4,3,1:T(8,128)} reshape(f32[4,16,16,16,8,8]{1,0,3,5,4,2:T(4,128)} %bitcast.114) | data formatting | bytes 8388608 | tf_op jit(solution)/shard_map/reshape;reshape | solution.py:122
  526.6 12.4 %bitcast_add_fusion = f32[64,16,16,16,4]{0,2,4,1,3:T(8,128)S(1)} fusion(f32[64,16,16,16,4]{0,2,4,3,1:T(8,128)} %reshape_reshape.3, f32[16,64,64]{2,1,0:T(8,128)S(1)} %fusion.77, f32[16,64]{1,0:T(8,128)S(1)} %broadcast_divide_fusion, f32[16]{0:T(128)S(1)} %get-tuple-element.23, f32[16,16,16,4]{1,3,2,0:T(4,128)S(1)} %bitcast.122), kind=kOutput, calls=%fused_computation.8 | convolution fusion | flops 807534592 | bytes 8720448 | tf_op jit(solution)/shard_map/icxtr,tij->jcxtr/dot_general | solution.py:127
  538.9 4.1 copy.206
  543.0 10.4 %copy.207 = f32[64,16,16,64]{3,2,1,0:T(8,128)} copy(f32[64,16,16,64]{0,2,3,1:T(8,128)} %bitcast.121) | data formatting | bytes 8388608 | tf_op jit(solution)/shard_map/reshape | solution.py:128
  (68 shorter events, 21.4 us)
Async XLA Ops:
  10.8 18.1 %copy-start.4 = (f32[8,512]{1,0:T(8,128)S(1)}, f32[8,512]{1,0:T(8,128)}, u32[]{:S(2)}) copy-start(f32[8,512]{1,0:T(8,128)} %param.11) | copy-start | bytes 49156
  22.5 15.2 %copy-start = (f32[16,16,8,512]{3,2,1,0:T(8,128)S(1)}, f32[16,16,8,512]{3,2,1,0:T(8,128)}, u32[]{:S(2)}) copy-start(f32[16,16,8,512]{3,2,1,0:T(8,128)} %param.9) | copy-start | bytes 12582916
  22.5 268.8 %collective-permute-start.3 = (bf16[16,66,4096]{2,0,1:T(8,128)(2,1)}, bf16[16,66,4096]{2,0,1:T(8,128)(2,1)}, u32[]{:S(2)}, u32[]{:S(2)}) collective-permute-start(bf16[16,66,4096]{2,0,1:T(8,128)(2,1)} %copy.194), channel_id=1, source_target_pairs={{1,0},{2,1},{3,2},{4,3},{5,4},{6,5},{7,6},{8,7},{9,8},{10,9},{11,1... | collective-permute-start | bytes 25952264 | tf_op jit(solution)/shard_map/ppermute | solution.py:17
  28.9 274.3 %collective-permute-start.2 = (bf16[16,66,4096]{2,0,1:T(8,128)(2,1)}, bf16[16,66,4096]{2,0,1:T(8,128)(2,1)}, u32[]{:S(2)}, u32[]{:S(2)}) collective-permute-start(bf16[16,66,4096]{2,0,1:T(8,128)(2,1)} %copy.194), channel_id=1, source_target_pairs={{0,1},{1,2},{2,3},{3,4},{4,5},{5,6},{6,7},{7,8},{8,9},{9,10},{10,1... | collective-permute-start | bytes 25952264 | tf_op jit(solution)/shard_map/ppermute | solution.py:16
  32.8 21.0 %collective-permute-start = (f32[257,1,512]{2,1,0:T(1,128)S(1)}, f32[257,1,512]{2,1,0:T(1,128)}, u32[]{:S(2)}, u32[]{:S(2)}) collective-permute-start(f32[257,1,512]{2,1,0:T(1,128)S(1)} %get-tuple-element.7), channel_id=1, source_target_pairs={{0,1},{1,2},{2,3},{3,4},{4,5},{5,6},{6,7},{8,9},{9,10},{10,11},{11... | collective-permute-start | bytes 1579016 | tf_op jit(solution)/shard_map/ppermute | solution.py:16
  34.9 20.0 %collective-permute-start.1 = (f32[257,1,512]{2,1,0:T(1,128)S(1)}, f32[257,1,512]{2,1,0:T(1,128)S(1)}, u32[]{:S(2)}, u32[]{:S(2)}) collective-permute-start(f32[257,1,512]{2,1,0:T(1,128)S(1)} %get-tuple-element.8), channel_id=1, source_target_pairs={{1,0},{2,1},{3,2},{4,3},{5,4},{6,5},{7,6},{9,8},{10,9},{11,10},{12... | collective-permute-start | bytes 1579016 | tf_op jit(solution)/shard_map/ppermute | solution.py:17
  37.7 7.6 %copy-start.5 = (f32[8,512]{1,0:T(8,128)S(1)}, f32[8,512]{1,0:T(8,128)}, u32[]{:S(2)}) copy-start(f32[8,512]{1,0:T(8,128)} %param.10) | copy-start | bytes 49156
  42.3 3.4 copy-start.1
  50.8 2.9 copy-start.6
  50.8 3.0 copy-start.7
  120.8 265.6 %all-to-all-start = ((f32[32,1,32768]{2,1,0:T(1,128)}), f32[32,1,32768]{2,1,0:T(1,128)}, u32[]{:S(2)}, u32[]{:S(2)}) async-start(f32[32,1,32768]{2,1,0:T(1,128)} %reshape.89), calls=%async_computation | async-start | bytes 8388608 | tf_op jit(solution)/shard_map/all_to_all | solution.py:93
  368.4 4.7 copy-start.2
  368.4 4.7 copy-start.3
where the time goes:
time: 562 us; the launch traced here: 554 us
  local copies, waits for them, and re-layouts  214 us (38%)
  starting transfers between devices  180 us (32%)
  other arithmetic  100 us (18%)
  matrix products  55.8 us (10%)
    all_to_all x1, starting transfers between devices, per_device(): lax.all_to_all(moved, ('mem', 'lat'), split_axis=3, concat_axis=0, tiled=...  170 us
    unnamed x20, local copies, waits for them, and re-layouts  58.7 us
    reshape x1, local copies, waits for them, and re-layouts, per_device(): arrived.reshape(mem_count, lat_count, members_dev, channels, lon_strip, r...  41.9 us
    reduce_sum x1, other arithmetic, per_device(): member_mean = jnp.mean(grid, axis=0)  29.4 us
    reshape x1, local copies, waits for them, and re-layouts, per_device(): moved = rows_last.reshape(1, members_dev, channels, lon_count, row_count)  26.4 us
    another operation x1, local copies, waits for them, and re-layouts, per_device(): arrived.reshape(members, channels, lon_strip, blocks_per_processor, lat_t...  25.7 us
    concatenate x2, other arithmetic, extended(): x = jnp.concatenate([before, x, after], axis=dim)  20.3 us
    dot_general x1, matrix products, tile_terms(): jnp.einsum('tko,tlo->tkl', weighted, perturb, preferred_element_type=jnp....  17.6 us
  transfers between devices with their start and end apart: 5, of which 1 were waited for; matrix products, arithmetic and copies ran while one was open for 33% of the time, Pallas kernels for 0%

commit v1 on v0

--- a/solution.py
+++ b/solution.py
@@ -1,9 +1,12 @@
 import jax
 import jax.numpy as jnp
 from jax import lax
+from jax.experimental import pallas as pl
+from jax.experimental.pallas import tpu as pltpu
 from jax.sharding import PartitionSpec as P
 
 NS_ITERS = 5
+VMEM_BYTES = 48 * 1024 * 1024
 
 
 def extended(x, sides, width, wrap):
@@ -48,7 +51,7 @@
     return spread_part + ensemble_mean_portion[:, :, None]
 
 
-def per_device(
+def general_device(
     prior_member_stack,
     zonal_stability_ratio,
     meridional_stability_ratio,
@@ -128,6 +131,324 @@
     return (member_mean + update).reshape(members, channels, lon_strip, lat_total)
 
 
+def swap_lane_groups(blocks, lane):
+    blocks = list(blocks)
+    count = len(blocks)
+    width = lane.shape[1] // count
+    bit = 1
+    while bit < count:
+        keep = (lane // width) & bit == 0
+        for k in range(count):
+            if k & bit == 0:
+                a, b = blocks[k], blocks[k | bit]
+                blocks[k] = jnp.where(keep, a, pltpu.roll(b, bit * width, 1))
+                blocks[k | bit] = jnp.where(keep, pltpu.roll(a, lane.shape[1] - bit * width, 1), b)
+        bit *= 2
+    return blocks
+
+
+def advance_kernel(prior_ref, zonal_ref, north_ref, south_c_ref, below_ref, above_ref, out_ref):
+    pair, channels, rows, lons = prior_ref.shape
+    zonal, north = zonal_ref[...], north_ref[...]
+    z_pos, z_neg = jnp.maximum(zonal, 0.0), jnp.minimum(zonal, 0.0)
+    n_pos, n_neg = jnp.maximum(north, 0.0), jnp.minimum(north, 0.0)
+    south = south_c_ref[...]
+    s_pos, s_neg = jnp.maximum(south, 0.0), jnp.minimum(south, 0.0)
+    row = lax.broadcasted_iota(jnp.int32, (rows, lons), 0)
+    lane = lax.broadcasted_iota(jnp.int32, (pair * rows, 128), 1)
+
+    def advanced(i, c):
+        p = prior_ref[i, c]
+        east = pltpu.roll(p, lons - 1, 1)
+        fe = z_pos * p + z_neg * east
+        above = jnp.where(row == rows - 1, above_ref[i, c : c + 1, :], pltpu.roll(p, rows - 1, 0))
+        fn = n_pos * p + n_neg * above
+        face = s_pos * below_ref[i, c : c + 1, :] + s_neg * p[0:1]
+        fs = jnp.where(row == 0, face, pltpu.roll(fn, 1, 0))
+        return p - (fe - pltpu.roll(fe, 1, 1)) - (fn - fs)
+
+    for h in range(channels // 8):
+        whole = [
+            jnp.concatenate([advanced(i, 8 * h + k) for i in range(pair)], axis=0)
+            for k in range(8)
+        ]
+        for q in range(lons // 128):
+            moved = swap_lane_groups([w[:, q * 128 : (q + 1) * 128] for w in whole], lane)
+            for s in range(8):
+                out_ref[q * 8 + s, :, h * 128 : (h + 1) * 128] = moved[s].astype(jnp.bfloat16)
+
+
+def gram_kernel(perturb_ref, innovation_ref, variance_ref, count_ref, out_ref):
+    t = pl.program_id(0)
+    perturb = perturb_ref[0]
+    members, slots = perturb.shape
+    valid = lax.broadcasted_iota(jnp.int32, (1, slots), 1) < count_ref[t]
+    variance = variance_ref[pl.ds(t, 1), :]
+    weight = jnp.where(valid, variance, 0.0).astype(jnp.bfloat16)
+    drive = jnp.where(valid, variance * innovation_ref[pl.ds(t, 1), :], 0.0).astype(jnp.bfloat16)
+    weighted = (perturb.astype(jnp.float32) * weight.astype(jnp.float32)).astype(jnp.bfloat16)
+    first = lax.broadcasted_iota(jnp.int32, (16, slots), 0) == 0
+    extra = jnp.where(first, drive.astype(jnp.float32), 0.0).astype(jnp.bfloat16)
+    left = jnp.concatenate([weighted, extra], axis=0)
+    both = lax.dot_general(
+        left, perturb, (((1,), (1,)), ((), ())), preferred_element_type=jnp.float32
+    )
+    out_ref[0] = both[: members + 8]
+
+
+def split(x):
+    hi = x.astype(jnp.bfloat16)
+    return hi, (x - hi.astype(jnp.float32)).astype(jnp.bfloat16)
+
+
+def dot(a, b):
+    return jnp.dot(a, b, preferred_element_type=jnp.float32)
+
+
+def analysis_kernel(bands, rows, tile_rows, weights_ref, arrived_ref, out_ref, held):
+    step = pl.program_id(0)
+    members = weights_ref.shape[1]
+    wide = members * rows
+    per_band = rows // tile_rows
+
+    @pl.when(step < bands)
+    def _():
+        pick_row = lax.broadcasted_iota(jnp.int32, (wide, per_band * members), 0)
+        pick_col = lax.broadcasted_iota(jnp.int32, (wide, per_band * members), 1)
+        source = (pick_row % rows) // tile_rows * members + pick_row // rows
+        pick = jnp.where(pick_col == source, 1.0, 0.0).astype(jnp.bfloat16)
+        spread_row = lax.broadcasted_iota(jnp.int32, (members, wide), 0)
+        spread_col = lax.broadcasted_iota(jnp.int32, (members, wide), 1)
+        spread = jnp.where(spread_col // rows == spread_row, 1.0, 0.0).astype(jnp.bfloat16)
+        here = lax.broadcasted_iota(jnp.int32, (wide, wide), 0) % rows
+        there = lax.broadcasted_iota(jnp.int32, (wide, wide), 1) % rows
+        diagonal = here == there
+        mine = weights_ref[...].reshape(per_band * members, members)
+        fields = arrived_ref[...].reshape(wide, arrived_ref.shape[-1])
+        total = None
+        for part in split(mine):
+            tall = dot(pick, part).astype(jnp.bfloat16)
+            full = jnp.where(diagonal, dot(tall, spread), 0.0).astype(jnp.bfloat16)
+            term = dot(full, fields)
+            total = term if total is None else total + term
+        where = pl.ds(pl.multiple_of(step * rows, rows), rows)
+        held[:, where, :] = total.reshape(members, rows, fields.shape[-1])
+
+    @pl.when(step >= bands)
+    def _():
+        count, channels, strip, lat = out_ref.shape
+        for k in range(count):
+            j = (step - bands) * count + k
+            out_ref[k] = held[j].T.reshape(channels, strip, lat)
+
+
+def exchange_kernel(sent_ref, got_ref, local_sem, send_sems, recv_sems):
+    lat_count = lax.axis_size("lat")
+    count = lax.axis_size("mem") * lat_count
+    me = lax.axis_index("mem") * lat_count + lax.axis_index("lat")
+
+    def place(d):
+        return {"mem": d // lat_count, "lat": d % lat_count}
+
+    barrier = pltpu.get_barrier_semaphore()
+
+    def greet(k, carry):
+        pl.semaphore_signal(
+            barrier, inc=1, device_id=place((me + k) % count), device_id_type=pl.DeviceIdType.MESH
+        )
+        return carry
+
+    lax.fori_loop(1, count, greet, 0)
+    pl.semaphore_wait(barrier, count - 1)
+    own = pltpu.make_async_copy(sent_ref.at[me], got_ref.at[me], local_sem)
+    own.start()
+
+    def sending(k):
+        to = (me + k) % count
+        return pltpu.make_async_remote_copy(
+            src_ref=sent_ref.at[to],
+            dst_ref=got_ref.at[me],
+            send_sem=send_sems.at[k],
+            recv_sem=recv_sems.at[k],
+            device_id=place(to),
+            device_id_type=pl.DeviceIdType.MESH,
+        )
+
+    def arriving(k):
+        origin = (me - k + count) % count
+        return pltpu.make_async_remote_copy(
+            src_ref=sent_ref.at[origin],
+            dst_ref=got_ref.at[origin],
+            send_sem=send_sems.at[k],
+            recv_sem=recv_sems.at[k],
+            device_id=place(origin),
+            device_id_type=pl.DeviceIdType.MESH,
+        )
+
+    def begin(k, carry):
+        sending(k).start()
+        return carry
+
+    def finish(k, carry):
+        sending(k).wait_send()
+        arriving(k).wait_recv()
+        return carry
+
+    lax.fori_loop(1, count, begin, 0)
+    lax.fori_loop(1, count, finish, 0)
+    own.wait()
+
+
+def shifted(x, axis, wrap):
+    size = lax.axis_size(axis)
+    up = [(i, (i + 1) % size) for i in range(size if wrap else size - 1)]
+    down = [(j, i) for i, j in up]
+    return up, down
+
+
+def fast_device(
+    prior_member_stack,
+    zonal_stability_ratio,
+    meridional_stability_ratio,
+    obs_perturb,
+    innovation,
+    inverse_error_variance,
+    obs_count,
+    neighbours,
+    localization,
+):
+    members_dev, channels, row_count, lon_count = prior_member_stack.shape
+    mem_count = lax.axis_size("mem")
+    lat_count = lax.axis_size("lat")
+    devices = mem_count * lat_count
+    strip = lon_count // devices
+    members = members_dev * mem_count
+    lat_total = row_count * lat_count
+    tiles, slots = innovation.shape
+    neigh_count = neighbours.shape[1]
+    tile_rows = lat_total // tiles
+    params = pltpu.CompilerParams(vmem_limit_bytes=VMEM_BYTES)
+
+    up, down = shifted(prior_member_stack, "lat", False)
+    below = lax.ppermute(prior_member_stack[:, :, row_count - 1, :], "lat", up)
+    above = lax.ppermute(prior_member_stack[:, :, 0, :], "lat", down)
+    south_c = lax.ppermute(meridional_stability_ratio[row_count - 1 :], "lat", up)
+
+    gram = pl.pallas_call(
+        gram_kernel,
+        grid=(tiles,),
+        out_shape=jax.ShapeDtypeStruct((tiles, members + 8, members), jnp.float32),
+        in_specs=[
+            pl.BlockSpec((1, members, slots), lambda t: (t, 0, 0)),
+            pl.BlockSpec((tiles, slots), lambda t: (0, 0)),
+            pl.BlockSpec((tiles, slots), lambda t: (0, 0)),
+            pl.BlockSpec(memory_space=pltpu.SMEM),
+        ],
+        out_specs=pl.BlockSpec((1, members + 8, members), lambda t: (t, 0, 0)),
+        compiler_params=params,
+        name="gram",
+    )(obs_perturb, innovation, inverse_error_variance, obs_count)
+    ring = ("mem", "lat")
+    up, down = shifted(gram, ring, True)
+    window = jnp.concatenate(
+        [lax.ppermute(gram, ring, up), gram, lax.ppermute(gram, ring, down)], axis=0
+    )
+
+    pair = 2
+    sent = pl.pallas_call(
+        advance_kernel,
+        grid=(members_dev // pair,),
+        out_shape=jax.ShapeDtypeStruct(
+            (devices, members_dev * row_count, channels * strip), jnp.bfloat16
+        ),
+        in_specs=[
+            pl.BlockSpec((pair, channels, row_count, lon_count), lambda g: (g, 0, 0, 0)),
+            pl.BlockSpec((row_count, lon_count), lambda g: (0, 0)),
+            pl.BlockSpec((row_count, lon_count), lambda g: (0, 0)),
+            pl.BlockSpec((1, lon_count), lambda g: (0, 0)),
+            pl.BlockSpec((pair, channels, lon_count), lambda g: (g, 0, 0)),
+            pl.BlockSpec((pair, channels, lon_count), lambda g: (g, 0, 0)),
+        ],
+        out_specs=pl.BlockSpec((devices, pair * row_count, channels * strip), lambda g: (0, g, 0)),
+        compiler_params=params,
+        name="advance",
+    )(
+        prior_member_stack,
+        zonal_stability_ratio,
+        meridional_stability_ratio,
+        south_c,
+        below,
+        above,
+    )
+
+    arrived = pl.pallas_call(
+        exchange_kernel,
+        out_shape=jax.ShapeDtypeStruct(sent.shape, sent.dtype),
+        in_specs=[pl.BlockSpec(memory_space=pl.ANY)],
+        out_specs=pl.BlockSpec(memory_space=pl.ANY),
+        scratch_shapes=[
+            pltpu.SemaphoreType.DMA(()),
+            pltpu.SemaphoreType.DMA((devices,)),
+            pltpu.SemaphoreType.DMA((devices,)),
+        ],
+        compiler_params=pltpu.CompilerParams(collective_id=0, has_side_effects=True),
+        name="exchange",
+    )(sent)
+
+    window_slots = lax.broadcasted_iota(jnp.int32, (tiles, 3 * tiles), 1)
+    combine = jnp.zeros((tiles, 3 * tiles), jnp.float32)
+    for n in range(neigh_count):
+        combine = combine + jnp.where(
+            neighbours[:, n, None] == window_slots, localization[:, n, None], 0.0
+        )
+    gathered = jnp.einsum("ts,skl->tkl", combine, window, precision=lax.Precision.HIGHEST)
+    curvature = (members - 1.0) * jnp.eye(members, dtype=jnp.float32)[None] + gathered[:, :members]
+    weights = transform_weights(curvature, gathered[:, members], members)
+    folded = jnp.swapaxes(
+        1.0 / members + weights - jnp.mean(weights, axis=1, keepdims=True), 1, 2
+    )
+
+    per_band = row_count // tile_rows
+    j_block = 8
+    j_steps = members // j_block
+    last = lat_count - 1
+    return pl.pallas_call(
+        lambda *refs: analysis_kernel(lat_count, row_count, tile_rows, *refs),
+        grid=(lat_count + j_steps,),
+        out_shape=jax.ShapeDtypeStruct((members, channels, strip, lat_total), jnp.float32),
+        in_specs=[
+            pl.BlockSpec((per_band, members, members), lambda s: (jnp.minimum(s, last), 0, 0)),
+            pl.BlockSpec(
+                (mem_count, 1, members_dev * row_count, channels * strip),
+                lambda s: (0, jnp.minimum(s, last), 0, 0),
+            ),
+        ],
+        out_specs=pl.BlockSpec(
+            (j_block, channels, strip, lat_total),
+            lambda s: (jnp.maximum(s - lat_count, 0), 0, 0, 0),
+        ),
+        scratch_shapes=[pltpu.VMEM((members, lat_total, channels * strip), jnp.float32)],
+        compiler_params=params,
+        name="analysis",
+    )(folded, arrived.reshape(mem_count, lat_count, members_dev * row_count, channels * strip))
+
+
+def per_device(prior_member_stack, *rest):
+    members_dev, channels, row_count, lon_count = prior_member_stack.shape
+    lat_count = lax.axis_size("lat")
+    devices = lax.axis_size("mem") * lat_count
+    tiles = rest[3].shape[0]
+    tile_rows = row_count * lat_count // tiles
+    fits = (
+        lon_count == 16 * devices
+        and channels % 8 == 0
+        and row_count == 8
+        and tile_rows in (1, 2, 4, 8)
+        and members_dev % 2 == 0
+    )
+    return (fast_device if fits else general_device)(prior_member_stack, *rest)
+
+
 def solution(mesh):
     in_specs = (
         P("mem", None, "lat", None),

time: 562 us -> 148 us (0.26)
  local copies, waits for them, and re-layouts: 214 us -> 18 us
  starting transfers between devices: 180 us -> 10.4 us
  Pallas kernels: 0 us -> 99.9 us
  other arithmetic: 100 us -> 2.34 us
  matrix products: 55.8 us -> 13.4 us
    all_to_all x1 -> x0, starting transfers between devices: 170 us -> none  [per_device(): lax.all_to_all(moved, ('mem', 'lat'), split_axis=3, concat_axis=0, tiled=...]
    pallas_call x0 -> x4, Pallas kernels: none -> 99.9 us  [the longest x1 52.1 us: fast_device(): pl.pallas_call(exchange_kernel, out_shape=jax.ShapeDtypeStruct(sent.shape...]
    reshape x3 -> x0, local copies, waits for them, and re-layouts: 78.8 us -> none  [the longest x1 41.9 us: per_device(): arrived.reshape(mem_count, lat_count, members_dev, channels, lon_strip, r...]
    unnamed x20 -> x30, local copies, waits for them, and re-layouts: 58.7 us -> 7.18 us
    concatenate x7 -> x1, other arithmetic: 37.7 us -> 1.36 us  [fast_device(): jnp.concatenate([lax.ppermute(gram, ring, up), gram, lax.ppermute(gram, r...]
    dot_general x3 -> x1, matrix products: 31.7 us -> 2.28 us  [fast_device(): jnp.einsum('ts,skl->tkl', combine, window, precision=lax.Precision.HIGHEST)]
    reduce_sum x1, other arithmetic: 29.4 us -> 0.3 us  [fast_device(): jnp.mean(weights, axis=1, keepdims=True)]
    another operation x1 -> x0, local copies, waits for them, and re-layouts: 25.7 us -> none  [per_device(): arrived.reshape(members, channels, lon_strip, blocks_per_processor, lat_t...]
  transfers between devices with their start and end apart: 5 -> 5, of which waited for: 1 -> 1; matrix products, arithmetic and copies ran while one was open for 33% -> 19% of each run, Pallas kernels for 0% -> 0%
where the time goes in v1:
time: 148 us; the launch traced here: 145 us
  Pallas kernels  99.9 us (68%)
  local copies, waits for them, and re-layouts  18 us (12%)
  matrix products  13.4 us (9%)
  starting transfers between devices  10.4 us (7%)
  other arithmetic  2.34 us (2%)
    pallas_call x1, Pallas kernels, fast_device(): pl.pallas_call(exchange_kernel, out_shape=jax.ShapeDtypeStruct(sent.shape...  52.1 us
    pallas_call x1, Pallas kernels, fast_device(): pl.pallas_call(advance_kernel, grid=(members_dev // pair,), out_shape=jax...  21.7 us
    pallas_call x1, Pallas kernels, fast_device(): pl.pallas_call(lambda *refs: analysis_kernel(lat_count, row_count, tile_r...  14.3 us
    pallas_call x1, Pallas kernels, fast_device(): pl.pallas_call(gram_kernel, grid=(tiles,), out_shape=jax.ShapeDtypeStruct...  11.7 us
    unnamed x30, local copies, waits for them, and re-layouts  7.18 us
    ppermute x1, starting transfers between devices, fast_device(): lax.ppermute(gram, ring, down)  6.43 us
    slice x1, local copies, waits for them, and re-layouts, fast_device(): above = lax.ppermute(prior_member_stack[:, :, 0, :], 'lat', down)  4.6 us
    dot_general x5, matrix products, transform_weights(): jnp.einsum('tij,tjk->tik', inverse, current, precision=lax.Precision.HIGH...  3.22 us
  transfers between devices with their start and end apart: 5, of which 1 were waited for; matrix products, arithmetic and copies ran while one was open for 19% of the time, Pallas kernels for 0%

profile of v1, /device:TPU:0, one launch (start us, length us, event | category | flops | bytes accessed | tf_op | source)
XLA Modules:
  0.0 145.0 jit_solution(15875368568018441412)
XLA Ops:
  0.0 0.9 copy-done.2
  1.0 0.9 copy-done.3
  2.6 11.7 %gram.1 = f32[16,72,64]{2,1,0:T(8,128)S(1)} custom-call(bf16[16,64,4096]{2,1,0:T(8,128)(2,1)} %perturb_ref.1, f32[16,4096]{1,0:T(8,128)S(1)} %copy-done.2, f32[16,4096]{1,0:T(8,128)S(1)} %copy-done.3, s32[16]{0:T(128)S(1)} %copy-done.6), custom_call_target="tpu_custom_call" | custom-call | tf_op jit(solution)/shard_map/gram/pallas_call | solution.py:337
  14.5 6.4 %collective-permute-start.1 = (f32[16,72,64]{1,2,0:T(8,128)S(1)}, f32[16,72,64]{1,2,0:T(8,128)S(1)}, u32[]{:S(2)}, u32[]{:S(2)}) collective-permute-start(f32[16,72,64]{1,2,0:T(8,128)S(1)} %copy.27), channel_id=1, source_target_pairs={{1,0},{2,1},{3,2},{4,3},{5,4},{6,5},{7,6},{8,7},{9,8},{10,9},{11,1... | collective-permute-start | bytes 884744 | tf_op jit(solution)/shard_map/ppermute | solution.py:354
  21.5 1.4 collective-permute-start.2
  22.9 4.6 %fusion.40 = (f32[16,16,1,512]{3,2,1,0:T(1,128)S(1)}, f32[16,16,1,512]{3,2,1,0:T(1,128)S(1)}) fusion(f32[16,16,8,512]{3,2,1,0:T(8,128)} %prior_ref.1), kind=kLoop, calls=%fused_computation.75 | loop fusion | bytes 2097152 | tf_op jit(solution)/shard_map/slice | solution.py:334
  27.5 0.8 copy.49
  28.4 1.3 collective-permute-start.3
  29.7 0.8 copy.48
  30.5 1.3 collective-permute-start.4
  32.7 1.0 copy.30
  34.3 1.1 copy.29
  35.3 1.4 pad_maximum_fusion
  36.7 1.6 %copy.31 = f32[48,72,64]{1,0,2:T(8,128)} copy(f32[48,72,64]{2,1,0:T(8,128)S(1)} %pad_maximum_fusion) | data formatting | bytes 1769472 | tf_op jit(solution)/shard_map/concatenate | solution.py:353
  38.4 2.3 %fusion.13 = f32[16,72,64]{1,0,2:T(8,128)S(1)} fusion(f32[48,72,64]{1,0,2:T(8,128)} %copy.31, f32[16]{0:T(128)S(1)} %copy-done.12, s32[16]{0:T(128)S(1)} %get-tuple-element.11, f32[16]{0:T(128)S(1)} %copy-done.13, s32[16]{0:T(128)S(1)} %get-tuple-element.12, f32[16]{0:T(128)S(1)} %copy-done.9, s32[16]{0:T(128)S(1)} %get-tuple-element.8, ...), kind=kOutput, calls=%fused_computation.27 | convolution fusion | flops 42480384 | bytes 1180416 | tf_op jit(solution)/shard_map/ts,skl->tkl/dot_general | solution.py:404
  42.1 0.7 fusion.41
  43.4 0.7 fusion.3
  44.0 0.7 fusion.43
  44.7 0.7 fusion.42
  45.4 0.7 fusion.2
  46.0 0.7 fusion.45
  46.7 0.7 fusion.44
  47.3 0.7 fusion.1
  48.0 0.7 fusion.46
  49.6 0.7 fusion
  51.2 0.9 convolution_bitcast_fusion
  52.1 1.1 fusion.49
  53.9 21.7 %advance.1.sent_ref = bf16[32,128,256]{2,1,0:T(8,128)(2,1)S(1)} custom-call(f32[16,16,8,512]{3,2,1,0:T(8,128)} %prior_ref.1, f32[8,512]{1,0:T(8,128)S(1)} %copy-done.5, f32[8,512]{1,0:T(8,128)S(1)} %copy-done.4, f32[1,512]{1,0:T(1,128)S(1)} %collective-permute-done.2.south_c_ref, f32[16,16,512]{2,1,0:T(8,128)S(1)} %collective-permute-done.3.below_ref, ...), custom_call_target="tpu_custom_call" | custom-call | tf_op jit(solution)/shard_map/advance/pallas_call | solution.py:358
  75.6 1.3 copy-done
  76.9 52.1 %exchange.1 = bf16[32,128,256]{2,1,0:T(8,128)(2,1)} custom-call(bf16[32,128,256]{2,1,0:T(8,128)(2,1)} %copy-done), custom_call_target="tpu_custom_call" | custom-call | tf_op jit(solution)/shard_map/exchange/pallas_call | solution.py:384
  129.1 1.6 %copy-done.1 = bf16[32,128,256]{2,1,0:T(8,128)(2,1)S(1)} copy-done((bf16[32,128,256]{2,1,0:T(8,128)(2,1)S(1)}, bf16[32,128,256]{2,1,0:T(8,128)(2,1)}, u32[]{:S(2)}) %copy-start.1) | copy-done | bytes 2097176
  130.6 14.3 %analysis.1 = f32[64,16,16,64]{3,2,1,0:T(8,128)} custom-call(f32[16,64,64]{2,1,0:T(8,128)S(1)} %subtract_bitcast_fusion.refs_0_, bf16[4,8,128,256]{3,2,1,0:T(8,128)(2,1)S(1)} %bitcast.79), custom_call_target="tpu_custom_call" | custom-call | tf_op jit(solution)/shard_map/analysis/pallas_call | solution.py:415
  (54 shorter events, 7.2 us)
Async XLA Ops:
  0.0 0.9 copy-start.2
  1.0 0.9 copy-start.3
  1.9 0.7 copy-start.6
  2.6 18.4 %copy-start.4 = (f32[8,512]{1,0:T(8,128)S(1)}, f32[8,512]{1,0:T(8,128)}, u32[]{:S(2)}) copy-start(f32[8,512]{1,0:T(8,128)} %north_ref.1) | copy-start | bytes 49156
  14.5 18.2 %collective-permute-start.1 = (f32[16,72,64]{1,2,0:T(8,128)S(1)}, f32[16,72,64]{1,2,0:T(8,128)S(1)}, u32[]{:S(2)}, u32[]{:S(2)}) collective-permute-start(f32[16,72,64]{1,2,0:T(8,128)S(1)} %copy.27), channel_id=1, source_target_pairs={{1,0},{2,1},{3,2},{4,3},{5,4},{6,5},{7,6},{8,7},{9,8},{10,9},{11,1... | collective-permute-start | bytes 884744 | tf_op jit(solution)/shard_map/ppermute | solution.py:354
  20.9 13.3 %collective-permute-start = (f32[16,72,64]{1,2,0:T(8,128)S(1)}, f32[16,72,64]{1,2,0:T(8,128)S(1)}, u32[]{:S(2)}, u32[]{:S(2)}) collective-permute-start(f32[16,72,64]{1,2,0:T(8,128)S(1)} %copy.27), channel_id=1, source_target_pairs={{0,1},{1,2},{2,3},{3,4},{4,5},{5,6},{6,7},{7,8},{8,9},{9,10},{10,1... | collective-permute-start | bytes 884744 | tf_op jit(solution)/shard_map/ppermute | solution.py:354
  21.5 10.4 %copy-start.7 = (s32[16,6]{0,1:T(8,128)S(1)}, s32[16,6]{0,1:T(8,128)}, u32[]{:S(2)}) copy-start(s32[16,6]{0,1:T(8,128)} %param.16) | copy-start | bytes 1156
  21.5 10.6 %copy-start.8 = (f32[16,6]{0,1:T(8,128)S(1)}, f32[16,6]{0,1:T(8,128)}, u32[]{:S(2)}) copy-start(f32[16,6]{0,1:T(8,128)} %param.17) | copy-start | bytes 1156
  21.5 32.3 %collective-permute-start.2 = (f32[1,512]{1,0:T(1,128)}, f32[1,512]{1,0:T(1,128)S(1)}, u32[]{:S(2)}, u32[]{:S(2)}) collective-permute-start(f32[1,512]{1,0:T(1,128)} %slice.65), channel_id=1, source_target_pairs={{0,1},{1,2},{2,3},{3,4},{4,5},{5,6},{6,7},{8,9},{9,10},{10,11},{11... | collective-permute-start | bytes 6152 | tf_op jit(solution)/shard_map/ppermute | solution.py:335
  28.4 25.5 %collective-permute-start.3 = (f32[16,16,512]{2,1,0:T(8,128)}, f32[16,16,512]{2,1,0:T(8,128)S(1)}, u32[]{:S(2)}, u32[]{:S(2)}) collective-permute-start(f32[16,16,512]{2,1,0:T(8,128)} %bitcast.78), channel_id=1, source_target_pairs={{0,1},{1,2},{2,3},{3,4},{4,5},{5,6},{6,7},{8,9},{9,10},{10,11},{11... | collective-permute-start | bytes 1572872 | tf_op jit(solution)/shard_map/ppermute | solution.py:333
  30.5 23.3 %collective-permute-start.4 = (f32[16,16,512]{2,1,0:T(8,128)}, f32[16,16,512]{2,1,0:T(8,128)S(1)}, u32[]{:S(2)}, u32[]{:S(2)}) collective-permute-start(f32[16,16,512]{2,1,0:T(8,128)} %bitcast.77), channel_id=1, source_target_pairs={{1,0},{2,1},{3,2},{4,3},{5,4},{6,5},{7,6},{9,8},{10,9},{11,10},{12... | collective-permute-start | bytes 1572872 | tf_op jit(solution)/shard_map/ppermute | solution.py:334
  36.7 1.7 %copy-start.9 = (f32[16]{0:T(128)S(1)}, f32[16]{0:T(128)}, u32[]{:S(2)}) copy-start(f32[16]{0:T(128)} %get-tuple-element.14) | copy-start | bytes 196
  36.7 1.7 %copy-start.10 = (f32[16]{0:T(128)S(1)}, f32[16]{0:T(128)}, u32[]{:S(2)}) copy-start(f32[16]{0:T(128)} %get-tuple-element.15) | copy-start | bytes 196
  36.7 1.7 %copy-start.11 = (f32[16]{0:T(128)S(1)}, f32[16]{0:T(128)}, u32[]{:S(2)}) copy-start(f32[16]{0:T(128)} %get-tuple-element.16) | copy-start | bytes 196
  36.7 1.7 %copy-start.12 = (f32[16]{0:T(128)S(1)}, f32[16]{0:T(128)}, u32[]{:S(2)}) copy-start(f32[16]{0:T(128)} %get-tuple-element.17) | copy-start | bytes 196
  36.7 1.7 %copy-start.13 = (f32[16]{0:T(128)S(1)}, f32[16]{0:T(128)}, u32[]{:S(2)}) copy-start(f32[16]{0:T(128)} %get-tuple-element.18) | copy-start | bytes 196
  50.9 2.9 %copy-start.5 = (f32[8,512]{1,0:T(8,128)S(1)}, f32[8,512]{1,0:T(8,128)}, u32[]{:S(2)}) copy-start(f32[8,512]{1,0:T(8,128)} %zonal_ref.1) | copy-start | bytes 49156
  75.6 1.3 copy-start
  129.1 1.6 %copy-start.1 = (bf16[32,128,256]{2,1,0:T(8,128)(2,1)S(1)}, bf16[32,128,256]{2,1,0:T(8,128)(2,1)}, u32[]{:S(2)}) copy-start(bf16[32,128,256]{2,1,0:T(8,128)(2,1)} %exchange.1) | copy-start | bytes 6291460

commit v2 on v1

--- a/solution.py
+++ b/solution.py
@@ -147,7 +147,7 @@
     return blocks
 
 
-def advance_kernel(prior_ref, zonal_ref, north_ref, south_c_ref, below_ref, above_ref, out_ref):
+def advance(prior_ref, zonal_ref, north_ref, south_c_ref, below_ref, above_ref, out_ref, step):
     pair, channels, rows, lons = prior_ref.shape
     zonal, north = zonal_ref[...], north_ref[...]
     z_pos, z_neg = jnp.maximum(zonal, 0.0), jnp.minimum(zonal, 0.0)
@@ -156,6 +156,7 @@
     s_pos, s_neg = jnp.maximum(south, 0.0), jnp.minimum(south, 0.0)
     row = lax.broadcasted_iota(jnp.int32, (rows, lons), 0)
     lane = lax.broadcasted_iota(jnp.int32, (pair * rows, 128), 1)
+    where = pl.ds(pl.multiple_of(step * pair * rows, pair * rows), pair * rows)
 
     def advanced(i, c):
         p = prior_ref[i, c]
@@ -175,7 +176,7 @@
         for q in range(lons // 128):
             moved = swap_lane_groups([w[:, q * 128 : (q + 1) * 128] for w in whole], lane)
             for s in range(8):
-                out_ref[q * 8 + s, :, h * 128 : (h + 1) * 128] = moved[s].astype(jnp.bfloat16)
+                out_ref[q * 8 + s, where, h * 128 : (h + 1) * 128] = moved[s].astype(jnp.bfloat16)
 
 
 def gram_kernel(perturb_ref, innovation_ref, variance_ref, count_ref, out_ref):
@@ -242,64 +243,151 @@
             out_ref[k] = held[j].T.reshape(channels, strip, lat)
 
 
-def exchange_kernel(sent_ref, got_ref, local_sem, send_sems, recv_sems):
+def iterate(window, neighbours_ref, localization_ref, current, inverse, weights_ref):
+    tiles, members = weights_ref.shape[:2]
+    row = lax.broadcasted_iota(jnp.int32, (members, members), 0)
+    col = lax.broadcasted_iota(jnp.int32, (members, members), 1)
+    identity = jnp.where(row == col, 1.0, 0.0)
+
+    def exact(a, b, dims=((1,), (0,))):
+        return lax.dot_general(
+            a, b, (dims, ((), ())),
+            precision=lax.Precision.HIGHEST, preferred_element_type=jnp.float32,
+        )
+
+    scales, drives = [], []
+    for t in range(tiles):
+        total = None
+        for n in range(neighbours_ref.shape[1]):
+            term = localization_ref[t, n] * window[neighbours_ref[t, n]]
+            total = term if total is None else total + term
+        curvature = (members - 1.0) * identity + total[:members]
+        scale = jnp.sqrt(jnp.sum(curvature * curvature, keepdims=True))
+        scales.append(scale)
+        drives.append(total[members:])
+        current[t] = curvature / scale
+        inverse[t] = identity
+
+    def one(_, carry):
+        for t in range(tiles):
+            now, inv = current[t], inverse[t]
+            middle = 1.5 * identity - 0.5 * exact(inv, now)
+            current[t] = exact(now, middle)
+            inverse[t] = exact(middle, inv)
+        return carry
+
+    lax.fori_loop(0, NS_ITERS, one, 0)
+    for t in range(tiles):
+        inv = inverse[t]
+        half = exact(drives[t], inv, ((1,), (1,)))
+        shift = exact(half, inv, ((1,), (1,))) / scales[t]
+        turned = jnp.sqrt((members - 1.0) / scales[t]) * inv.T + shift[0:1]
+        weights_ref[t] = 1.0 / members + turned - jnp.mean(turned, axis=1, keepdims=True)
+
+
+def transport_kernel(
+    prior_ref, zonal_ref, north_ref, south_c_ref, below_ref, above_ref, gram_ref,
+    neighbours_ref, localization_ref, got_ref, weights_ref,
+    sent, window, current, inverse,
+    own_sem, gram_own_sem, send_sems, recv_sems, gram_send_sems, gram_recv_sems,
+):
+    step, steps = pl.program_id(0), pl.num_programs(0)
     lat_count = lax.axis_size("lat")
     count = lax.axis_size("mem") * lat_count
     me = lax.axis_index("mem") * lat_count + lax.axis_index("lat")
+    tiles = gram_ref.shape[0]
+    chunks = send_sems.shape[0]
+    per_chunk = steps // chunks
+    chunk_rows = sent.shape[1] // chunks
+    barrier = pltpu.get_barrier_semaphore()
 
     def place(d):
         return {"mem": d // lat_count, "lat": d % lat_count}
 
-    barrier = pltpu.get_barrier_semaphore()
-
-    def greet(k, carry):
-        pl.semaphore_signal(
-            barrier, inc=1, device_id=place((me + k) % count), device_id_type=pl.DeviceIdType.MESH
-        )
-        return carry
-
-    lax.fori_loop(1, count, greet, 0)
-    pl.semaphore_wait(barrier, count - 1)
-    own = pltpu.make_async_copy(sent_ref.at[me], got_ref.at[me], local_sem)
-    own.start()
-
-    def sending(k):
+    def sending(chunk, k):
         to = (me + k) % count
+        rows = pl.ds(pl.multiple_of(chunk * chunk_rows, chunk_rows), chunk_rows)
         return pltpu.make_async_remote_copy(
-            src_ref=sent_ref.at[to],
-            dst_ref=got_ref.at[me],
-            send_sem=send_sems.at[k],
-            recv_sem=recv_sems.at[k],
+            src_ref=sent.at[to, rows],
+            dst_ref=got_ref.at[me, rows],
+            send_sem=send_sems.at[chunk, k],
+            recv_sem=recv_sems.at[chunk, k],
             device_id=place(to),
             device_id_type=pl.DeviceIdType.MESH,
         )
 
-    def arriving(k):
+    def arriving(chunk, k):
         origin = (me - k + count) % count
+        rows = pl.ds(pl.multiple_of(chunk * chunk_rows, chunk_rows), chunk_rows)
         return pltpu.make_async_remote_copy(
-            src_ref=sent_ref.at[origin],
-            dst_ref=got_ref.at[origin],
-            send_sem=send_sems.at[k],
-            recv_sem=recv_sems.at[k],
+            src_ref=sent.at[origin, rows],
+            dst_ref=got_ref.at[origin, rows],
+            send_sem=send_sems.at[chunk, k],
+            recv_sem=recv_sems.at[chunk, k],
             device_id=place(origin),
             device_id_type=pl.DeviceIdType.MESH,
         )
 
-    def begin(k, carry):
-        sending(k).start()
-        return carry
-
-    def finish(k, carry):
-        sending(k).wait_send()
-        arriving(k).wait_recv()
-        return carry
-
-    lax.fori_loop(1, count, begin, 0)
-    lax.fori_loop(1, count, finish, 0)
-    own.wait()
-
-
-def shifted(x, axis, wrap):
+    def gram_copy(side):
+        to = (me + 1) % count if side == 0 else (me - 1 + count) % count
+        return pltpu.make_async_remote_copy(
+            src_ref=gram_ref,
+            dst_ref=window.at[pl.ds(2 * tiles * side, tiles)],
+            send_sem=gram_send_sems.at[side],
+            recv_sem=gram_recv_sems.at[side],
+            device_id=place(to),
+            device_id_type=pl.DeviceIdType.MESH,
+        )
+
+    gram_own = pltpu.make_async_copy(gram_ref, window.at[pl.ds(tiles, tiles)], gram_own_sem)
+    own = pltpu.make_async_copy(sent.at[me], got_ref.at[me], own_sem)
+
+    @pl.when(step == 0)
+    def _():
+        def greet(k, carry):
+            pl.semaphore_signal(
+                barrier, inc=1, device_id=place((me + k) % count),
+                device_id_type=pl.DeviceIdType.MESH,
+            )
+            return carry
+
+        lax.fori_loop(1, count, greet, 0)
+        pl.semaphore_wait(barrier, count - 1)
+        gram_copy(0).start()
+        gram_copy(1).start()
+        gram_own.start()
+
+    advance(
+        prior_ref, zonal_ref, north_ref, south_c_ref, below_ref, above_ref, sent, step
+    )
+
+    @pl.when(step % per_chunk == per_chunk - 1)
+    def _():
+        def begin(k, carry):
+            sending(step // per_chunk, k).start()
+            return carry
+
+        lax.fori_loop(1, count, begin, 0)
+
+    @pl.when(step == steps - 1)
+    def _():
+        own.start()
+        gram_own.wait()
+        gram_copy(0).wait()
+        gram_copy(1).wait()
+        iterate(window, neighbours_ref, localization_ref, current, inverse, weights_ref)
+
+        def finish(i, carry):
+            chunk, k = i // (count - 1), i % (count - 1) + 1
+            sending(chunk, k).wait_send()
+            arriving(chunk, k).wait_recv()
+            return carry
+
+        lax.fori_loop(0, chunks * (count - 1), finish, 0)
+        own.wait()
+
+
+def shifted(axis, wrap):
     size = lax.axis_size(axis)
     up = [(i, (i + 1) % size) for i in range(size if wrap else size - 1)]
     down = [(j, i) for i, j in up]
@@ -325,14 +413,19 @@
     members = members_dev * mem_count
     lat_total = row_count * lat_count
     tiles, slots = innovation.shape
-    neigh_count = neighbours.shape[1]
     tile_rows = lat_total // tiles
     params = pltpu.CompilerParams(vmem_limit_bytes=VMEM_BYTES)
 
-    up, down = shifted(prior_member_stack, "lat", False)
-    below = lax.ppermute(prior_member_stack[:, :, row_count - 1, :], "lat", up)
-    above = lax.ppermute(prior_member_stack[:, :, 0, :], "lat", down)
-    south_c = lax.ppermute(meridional_stability_ratio[row_count - 1 :], "lat", up)
+    up, down = shifted("lat", False)
+    edges = (
+        prior_member_stack[:, :, row_count - 1, :],
+        prior_member_stack[:, :, 0, :],
+        meridional_stability_ratio[row_count - 1 :],
+    )
+    *edges, obs_count = lax.optimization_barrier((*edges, obs_count))
+    below = lax.ppermute(edges[0], "lat", up)
+    above = lax.ppermute(edges[1], "lat", down)
+    south_c = lax.ppermute(edges[2], "lat", up)
 
     gram = pl.pallas_call(
         gram_kernel,
@@ -346,20 +439,21 @@
         ],
         out_specs=pl.BlockSpec((1, members + 8, members), lambda t: (t, 0, 0)),
         compiler_params=params,
+        cost_estimate=pl.CostEstimate(
+            flops=4 * obs_perturb.size * members, bytes_accessed=4 * obs_perturb.size, transcendentals=0
+        ),
         name="gram",
     )(obs_perturb, innovation, inverse_error_variance, obs_count)
-    ring = ("mem", "lat")
-    up, down = shifted(gram, ring, True)
-    window = jnp.concatenate(
-        [lax.ppermute(gram, ring, up), gram, lax.ppermute(gram, ring, down)], axis=0
-    )
-
-    pair = 2
-    sent = pl.pallas_call(
-        advance_kernel,
+
+    pair, chunks = 2, 4
+    wire = (devices, members_dev * row_count, channels * strip)
+    square = (tiles, members, members)
+    arrived, folded = pl.pallas_call(
+        transport_kernel,
         grid=(members_dev // pair,),
-        out_shape=jax.ShapeDtypeStruct(
-            (devices, members_dev * row_count, channels * strip), jnp.bfloat16
+        out_shape=(
+            jax.ShapeDtypeStruct(wire, jnp.bfloat16),
+            jax.ShapeDtypeStruct(square, jnp.float32),
         ),
         in_specs=[
             pl.BlockSpec((pair, channels, row_count, lon_count), lambda g: (g, 0, 0, 0)),
@@ -368,10 +462,30 @@
             pl.BlockSpec((1, lon_count), lambda g: (0, 0)),
             pl.BlockSpec((pair, channels, lon_count), lambda g: (g, 0, 0)),
             pl.BlockSpec((pair, channels, lon_count), lambda g: (g, 0, 0)),
+            pl.BlockSpec(memory_space=pltpu.VMEM),
+            pl.BlockSpec(memory_space=pltpu.SMEM),
+            pl.BlockSpec(memory_space=pltpu.SMEM),
         ],
-        out_specs=pl.BlockSpec((devices, pair * row_count, channels * strip), lambda g: (0, g, 0)),
-        compiler_params=params,
-        name="advance",
+        out_specs=(
+            pl.BlockSpec(memory_space=pl.ANY),
+            pl.BlockSpec(square, lambda g: (0, 0, 0)),
+        ),
+        scratch_shapes=[
+            pltpu.VMEM(wire, jnp.bfloat16),
+            pltpu.VMEM((3 * tiles, members + 8, members), jnp.float32),
+            pltpu.VMEM(square, jnp.float32),
+            pltpu.VMEM(square, jnp.float32),
+            pltpu.SemaphoreType.DMA(()),
+            pltpu.SemaphoreType.DMA(()),
+            pltpu.SemaphoreType.DMA((chunks, devices)),
+            pltpu.SemaphoreType.DMA((chunks, devices)),
+            pltpu.SemaphoreType.DMA((2,)),
+            pltpu.SemaphoreType.DMA((2,)),
+        ],
+        compiler_params=pltpu.CompilerParams(
+            collective_id=0, has_side_effects=True, vmem_limit_bytes=VMEM_BYTES
+        ),
+        name="transport",
     )(
         prior_member_stack,
         zonal_stability_ratio,
@@ -379,33 +493,9 @@
         south_c,
         below,
         above,
-    )
-
-    arrived = pl.pallas_call(
-        exchange_kernel,
-        out_shape=jax.ShapeDtypeStruct(sent.shape, sent.dtype),
-        in_specs=[pl.BlockSpec(memory_space=pl.ANY)],
-        out_specs=pl.BlockSpec(memory_space=pl.ANY),
-        scratch_shapes=[
-            pltpu.SemaphoreType.DMA(()),
-            pltpu.SemaphoreType.DMA((devices,)),
-            pltpu.SemaphoreType.DMA((devices,)),
-        ],
-        compiler_params=pltpu.CompilerParams(collective_id=0, has_side_effects=True),
-        name="exchange",
-    )(sent)
-
-    window_slots = lax.broadcasted_iota(jnp.int32, (tiles, 3 * tiles), 1)
-    combine = jnp.zeros((tiles, 3 * tiles), jnp.float32)
-    for n in range(neigh_count):
-        combine = combine + jnp.where(
-            neighbours[:, n, None] == window_slots, localization[:, n, None], 0.0
-        )
-    gathered = jnp.einsum("ts,skl->tkl", combine, window, precision=lax.Precision.HIGHEST)
-    curvature = (members - 1.0) * jnp.eye(members, dtype=jnp.float32)[None] + gathered[:, :members]
-    weights = transform_weights(curvature, gathered[:, members], members)
-    folded = jnp.swapaxes(
-        1.0 / members + weights - jnp.mean(weights, axis=1, keepdims=True), 1, 2
+        gram,
+        neighbours,
+        localization,
     )
 
     per_band = row_count // tile_rows
@@ -444,7 +534,7 @@
         and channels % 8 == 0
         and row_count == 8
         and tile_rows in (1, 2, 4, 8)
-        and members_dev % 2 == 0
+        and members_dev % 8 == 0
     )
     return (fast_device if fits else general_device)(prior_member_stack, *rest)
 

time: 148 us -> 110 us (0.74); the launches traced: 145 us -> 110 us
  matrix products: 13.4 us -> 0 us
  local copies, waits for them, and re-layouts: 18 us -> 5.69 us
  Pallas kernels: 99.9 us -> 94.7 us
  other arithmetic: 2.34 us -> 0 us
    dot_general x17 -> x0, matrix products: 13.4 us -> none  [the longest x5 3.22 us: transform_weights(): jnp.einsum('tij,tjk->tik', inverse, current, precision=lax.Precision.HIGH...]
    unnamed x30 -> x16, local copies, waits for them, and re-layouts: 7.18 us -> 0.2 us
    pallas_call x2 -> x1, Pallas kernels: 73.8 us -> 68.6 us  [fast_device(): pl.pallas_call(transport_kernel, grid=(members_dev // pair,), out_shape=(...]
    ppermute x2 -> x0, local copies, waits for them, and re-layouts: 2.1 us -> none  [the longest x1 1.06 us: fast_device(): lax.ppermute(gram, ring, up)]
    concatenate x1 -> x0, local copies, waits for them, and re-layouts: 1.62 us -> none  [fast_device(): jnp.concatenate([lax.ppermute(gram, ring, up), gram, lax.ppermute(gram, r...]
    ppermute x5 -> x3, starting transfers between devices: 10.4 us -> 9.01 us  [the longest x1 5.19 us: fast_device(): south_c = lax.ppermute(edges[2], 'lat', up)]
    slice x3 -> x1, local copies, waits for them, and re-layouts: 5.08 us -> 4.6 us  [fast_device(): prior_member_stack[:, :, 0, :]]
  transfers between devices with their start and end apart: 5 -> 3, of which waited for: 1 -> 0; matrix products, arithmetic and copies ran while one was open for 19% -> 0% of each run, Pallas kernels for 0% -> 11%
where the time goes in v2:
time: 110 us
  Pallas kernels  94.7 us (86%)
  starting transfers between devices  9.01 us (8%)
  local copies, waits for them, and re-layouts  5.69 us (5%)
    pallas_call x1, Pallas kernels, fast_device(): pl.pallas_call(transport_kernel, grid=(members_dev // pair,), out_shape=(...  68.6 us
    pallas_call x1, Pallas kernels, fast_device(): pl.pallas_call(lambda *refs: analysis_kernel(lat_count, row_count, tile_r...  14.4 us
    pallas_call x1, Pallas kernels, fast_device(): pl.pallas_call(gram_kernel, grid=(tiles,), out_shape=jax.ShapeDtypeStruct...  11.7 us
    ppermute x1, starting transfers between devices, fast_device(): south_c = lax.ppermute(edges[2], 'lat', up)  5.19 us
    slice x1, local copies, waits for them, and re-layouts, fast_device(): prior_member_stack[:, :, 0, :]  4.6 us
    ppermute x1, starting transfers between devices, fast_device(): below = lax.ppermute(edges[0], 'lat', up)  2.53 us
  transfers between devices with their start and end apart: 3, of which 0 were waited for; matrix products, arithmetic and copies ran while one was open for 0% of the time, Pallas kernels for 11%

profile of v2, /device:TPU:0, one launch (start us, length us, event | category | flops | bytes accessed | tf_op | source)
XLA Modules:
  0.0 109.5 jit_solution(17513396867437746587)
XLA Ops:
  0.0 0.0 copy-start.4
  0.0 0.0 copy-start.1
  0.0 0.0 copy-start
  0.0 0.8 slice.11
  0.8 4.6 %fusion = (f32[16,16,1,512]{3,2,1,0:T(1,128)S(1)}, f32[16,16,1,512]{3,2,1,0:T(1,128)S(1)}) fusion(f32[16,16,8,512]{3,2,1,0:T(8,128)} %prior_ref.1), kind=kLoop, calls=%fused_computation.2 | loop fusion | bytes 2097152 | tf_op jit(solution)/shard_map/slice | solution.py:422
  5.4 0.1 copy_bitcast_fusion
  5.5 0.0 copy-start.5
  5.5 0.0 copy-start.6
  5.5 0.0 copy-start.2
  5.5 0.0 copy-start.3
  5.6 2.5 %collective-permute-start.1 = (f32[16,16,512]{2,1,0:T(8,128)S(1)}, f32[16,16,512]{2,1,0:T(8,128)S(1)}, u32[]{:S(2)}, u32[]{:S(2)}) collective-permute-start(f32[16,16,512]{2,1,0:T(8,128)S(1)} %get-tuple-element.12), channel_id=1, source_target_pairs={{0,1},{1,2},{2,3},{3,4},{4,5},{5,6},{6,7},{8,9},{9,10},{10,11},{11... | collective-permute-start | bytes 1572872 | tf_op jit(solution)/shard_map/ppermute | solution.py:426
  8.1 1.3 %collective-permute-start.2 = (f32[16,16,512]{2,1,0:T(8,128)S(1)}, f32[16,16,512]{2,1,0:T(8,128)S(1)}, u32[]{:S(2)}, u32[]{:S(2)}) collective-permute-start(f32[16,16,512]{2,1,0:T(8,128)S(1)} %get-tuple-element.13), channel_id=1, source_target_pairs={{1,0},{2,1},{3,2},{4,3},{5,4},{6,5},{7,6},{9,8},{10,9},{11,10},{12... | collective-permute-start | bytes 1572872 | tf_op jit(solution)/shard_map/ppermute | solution.py:427
  9.4 5.2 %collective-permute-start = (f32[1,512]{1,0:T(1,128)S(1)}, f32[1,512]{1,0:T(1,128)S(1)}, u32[]{:S(2)}, u32[]{:S(2)}) collective-permute-start(f32[1,512]{1,0:T(1,128)S(1)} %slice.11), channel_id=1, source_target_pairs={{0,1},{1,2},{2,3},{3,4},{4,5},{5,6},{6,7},{8,9},{9,10},{10,11},{11... | collective-permute-start | bytes 6152 | tf_op jit(solution)/shard_map/ppermute | solution.py:428
  14.6 0.0 copy-done.4
  14.6 0.0 copy-done.1
  14.6 0.0 copy-done
  14.6 11.7 %gram.1.gram_ref = f32[16,72,64]{2,1,0:T(8,128)S(1)} custom-call(bf16[16,64,4096]{2,1,0:T(8,128)(2,1)} %perturb_ref.1, f32[16,4096]{1,0:T(8,128)S(1)} %copy-done, f32[16,4096]{1,0:T(8,128)S(1)} %copy-done.1, s32[16]{0:T(128)S(1)} %copy-done.4), custom_call_target="tpu_custom_call" | custom-call | flops 1073741824 | bytes 16777216 | tf_op jit(solution)/shard_map/gram/pallas_call | solution.py:430
  26.3 0.0 copy-done.5
  26.4 0.1 copy.12.neighbours_ref
  26.4 0.0 copy-done.6
  26.4 0.1 copy.13.localization_ref
  26.5 0.0 collective-permute-done.south_c_ref
  26.5 0.0 collective-permute-done.1.below_ref
  26.5 0.0 collective-permute-done.2.above_ref
  26.5 0.0 copy-done.2
  26.5 0.0 copy-done.3
  26.6 68.6 %transport.1 = (bf16[32,128,256]{2,1,0:T(8,128)(2,1)S(1)}, f32[16,64,64]{2,1,0:T(8,128)S(1)}) custom-call(f32[16,16,8,512]{3,2,1,0:T(8,128)} %prior_ref.1, f32[8,512]{1,0:T(8,128)S(1)} %copy-done.3, f32[8,512]{1,0:T(8,128)S(1)} %copy-done.2, f32[1,512]{1,0:T(1,128)S(1)} %collective-permute-done.south_c_ref, ...), custom_call_target="tpu_custom_call" | custom-call | tf_op jit(solution)/shard_map/transport/pallas_call | solution.py:451
  95.2 14.4 %analysis.1 = f32[64,16,16,64]{3,2,1,0:T(8,128)} custom-call(f32[16,64,64]{2,1,0:T(8,128)S(1)} %get-tuple-element.15.refs_0_, bf16[4,8,128,256]{3,2,1,0:T(8,128)(2,1)S(1)} %bitcast.5), custom_call_target="tpu_custom_call" | custom-call | tf_op jit(solution)/shard_map/analysis/pallas_call | solution.py:505
Async XLA Ops:
  0.0 14.6 %copy-start.4 = (s32[16]{0:T(128)S(1)}, s32[16]{0:T(128)}, u32[]{:S(2)}) copy-start(s32[16]{0:T(128)} %count_ref) | copy-start | bytes 196
  0.0 14.6 %copy-start.1 = (f32[16,4096]{1,0:T(8,128)S(1)}, f32[16,4096]{1,0:T(8,128)}, u32[]{:S(2)}) copy-start(f32[16,4096]{1,0:T(8,128)} %variance_ref.1) | copy-start | bytes 786436
  0.0 14.6 %copy-start = (f32[16,4096]{1,0:T(8,128)S(1)}, f32[16,4096]{1,0:T(8,128)}, u32[]{:S(2)}) copy-start(f32[16,4096]{1,0:T(8,128)} %innovation_ref.1) | copy-start | bytes 786436
  5.5 20.8 %copy-start.5 = (s32[16,6]{0,1:T(8,128)S(1)}, s32[16,6]{0,1:T(8,128)}, u32[]{:S(2)}) copy-start(s32[16,6]{0,1:T(8,128)} %param.16) | copy-start | bytes 1156
  5.5 20.9 %copy-start.6 = (f32[16,6]{0,1:T(8,128)S(1)}, f32[16,6]{0,1:T(8,128)}, u32[]{:S(2)}) copy-start(f32[16,6]{0,1:T(8,128)} %param.17) | copy-start | bytes 1156
  5.5 21.0 %copy-start.2 = (f32[8,512]{1,0:T(8,128)S(1)}, f32[8,512]{1,0:T(8,128)}, u32[]{:S(2)}) copy-start(f32[8,512]{1,0:T(8,128)} %north_ref.1) | copy-start | bytes 49156
  5.5 21.0 %copy-start.3 = (f32[8,512]{1,0:T(8,128)S(1)}, f32[8,512]{1,0:T(8,128)}, u32[]{:S(2)}) copy-start(f32[8,512]{1,0:T(8,128)} %zonal_ref.1) | copy-start | bytes 49156
  5.6 21.0 %collective-permute-start.1 = (f32[16,16,512]{2,1,0:T(8,128)S(1)}, f32[16,16,512]{2,1,0:T(8,128)S(1)}, u32[]{:S(2)}, u32[]{:S(2)}) collective-permute-start(f32[16,16,512]{2,1,0:T(8,128)S(1)} %get-tuple-element.12), channel_id=1, source_target_pairs={{0,1},{1,2},{2,3},{3,4},{4,5},{5,6},{6,7},{8,9},{9,10},{10,11},{11... | collective-permute-start | bytes 1572872 | tf_op jit(solution)/shard_map/ppermute | solution.py:426
  8.1 18.4 %collective-permute-start.2 = (f32[16,16,512]{2,1,0:T(8,128)S(1)}, f32[16,16,512]{2,1,0:T(8,128)S(1)}, u32[]{:S(2)}, u32[]{:S(2)}) collective-permute-start(f32[16,16,512]{2,1,0:T(8,128)S(1)} %get-tuple-element.13), channel_id=1, source_target_pairs={{1,0},{2,1},{3,2},{4,3},{5,4},{6,5},{7,6},{9,8},{10,9},{11,10},{12... | collective-permute-start | bytes 1572872 | tf_op jit(solution)/shard_map/ppermute | solution.py:427
  9.4 17.1 %collective-permute-start = (f32[1,512]{1,0:T(1,128)S(1)}, f32[1,512]{1,0:T(1,128)S(1)}, u32[]{:S(2)}, u32[]{:S(2)}) collective-permute-start(f32[1,512]{1,0:T(1,128)S(1)} %slice.11), channel_id=1, source_target_pairs={{0,1},{1,2},{2,3},{3,4},{4,5},{5,6},{6,7},{8,9},{9,10},{10,11},{11... | collective-permute-start | bytes 6152 | tf_op jit(solution)/shard_map/ppermute | solution.py:428

commit v3 on v2

--- a/solution.py
+++ b/solution.py
@@ -152,7 +152,7 @@
     zonal, north = zonal_ref[...], north_ref[...]
     z_pos, z_neg = jnp.maximum(zonal, 0.0), jnp.minimum(zonal, 0.0)
     n_pos, n_neg = jnp.maximum(north, 0.0), jnp.minimum(north, 0.0)
-    south = south_c_ref[...]
+    south = south_c_ref[0:1]
     s_pos, s_neg = jnp.maximum(south, 0.0), jnp.minimum(south, 0.0)
     row = lax.broadcasted_iota(jnp.int32, (rows, lons), 0)
     lane = lax.broadcasted_iota(jnp.int32, (pair * rows, 128), 1)
@@ -162,9 +162,9 @@
         p = prior_ref[i, c]
         east = pltpu.roll(p, lons - 1, 1)
         fe = z_pos * p + z_neg * east
-        above = jnp.where(row == rows - 1, above_ref[i, c : c + 1, :], pltpu.roll(p, rows - 1, 0))
+        above = jnp.where(row == rows - 1, above_ref[i * channels + c : i * channels + c + 1, :], pltpu.roll(p, rows - 1, 0))
         fn = n_pos * p + n_neg * above
-        face = s_pos * below_ref[i, c : c + 1, :] + s_neg * p[0:1]
+        face = s_pos * below_ref[i * channels + c : i * channels + c + 1, :] + s_neg * p[0:1]
         fs = jnp.where(row == 0, face, pltpu.roll(fn, 1, 0))
         return p - (fe - pltpu.roll(fe, 1, 1)) - (fn - fs)
 
@@ -187,7 +187,7 @@
     variance = variance_ref[pl.ds(t, 1), :]
     weight = jnp.where(valid, variance, 0.0).astype(jnp.bfloat16)
     drive = jnp.where(valid, variance * innovation_ref[pl.ds(t, 1), :], 0.0).astype(jnp.bfloat16)
-    weighted = (perturb.astype(jnp.float32) * weight.astype(jnp.float32)).astype(jnp.bfloat16)
+    weighted = perturb * weight
     first = lax.broadcasted_iota(jnp.int32, (16, slots), 0) == 0
     extra = jnp.where(first, drive.astype(jnp.float32), 0.0).astype(jnp.bfloat16)
     left = jnp.concatenate([weighted, extra], axis=0)
@@ -216,20 +216,22 @@
     def _():
         pick_row = lax.broadcasted_iota(jnp.int32, (wide, per_band * members), 0)
         pick_col = lax.broadcasted_iota(jnp.int32, (wide, per_band * members), 1)
-        source = (pick_row % rows) // tile_rows * members + pick_row // rows
+        row_bits, tile_bits = rows.bit_length() - 1, tile_rows.bit_length() - 1
+        source = (((pick_row & (rows - 1)) >> tile_bits) * members) + (pick_row >> row_bits)
         pick = jnp.where(pick_col == source, 1.0, 0.0).astype(jnp.bfloat16)
         spread_row = lax.broadcasted_iota(jnp.int32, (members, wide), 0)
         spread_col = lax.broadcasted_iota(jnp.int32, (members, wide), 1)
-        spread = jnp.where(spread_col // rows == spread_row, 1.0, 0.0).astype(jnp.bfloat16)
-        here = lax.broadcasted_iota(jnp.int32, (wide, wide), 0) % rows
-        there = lax.broadcasted_iota(jnp.int32, (wide, wide), 1) % rows
+        spread = jnp.where((spread_col >> row_bits) == spread_row, 1.0, 0.0).astype(jnp.bfloat16)
+        here = lax.broadcasted_iota(jnp.int32, (1, rows, wide), 1)
+        there = lax.broadcasted_iota(jnp.int32, (1, rows, wide), 2) & (rows - 1)
         diagonal = here == there
         mine = weights_ref[...].reshape(per_band * members, members)
         fields = arrived_ref[...].reshape(wide, arrived_ref.shape[-1])
         total = None
         for part in split(mine):
             tall = dot(pick, part).astype(jnp.bfloat16)
-            full = jnp.where(diagonal, dot(tall, spread), 0.0).astype(jnp.bfloat16)
+            full = jnp.where(diagonal, dot(tall, spread).reshape(members, rows, wide), 0.0)
+            full = full.reshape(wide, wide).astype(jnp.bfloat16)
             term = dot(full, fields)
             total = term if total is None else total + term
         where = pl.ds(pl.multiple_of(step * rows, rows), rows)
@@ -417,15 +419,19 @@
     params = pltpu.CompilerParams(vmem_limit_bytes=VMEM_BYTES)
 
     up, down = shifted("lat", False)
+    halo = members_dev * channels
     edges = (
-        prior_member_stack[:, :, row_count - 1, :],
-        prior_member_stack[:, :, 0, :],
-        meridional_stability_ratio[row_count - 1 :],
+        jnp.concatenate(
+            [
+                prior_member_stack[:, :, row_count - 1, :].reshape(halo, lon_count),
+                jnp.broadcast_to(meridional_stability_ratio[row_count - 1 :], (8, lon_count)),
+            ]
+        ),
+        prior_member_stack[:, :, 0, :].reshape(halo, lon_count),
     )
     *edges, obs_count = lax.optimization_barrier((*edges, obs_count))
     below = lax.ppermute(edges[0], "lat", up)
     above = lax.ppermute(edges[1], "lat", down)
-    south_c = lax.ppermute(edges[2], "lat", up)
 
     gram = pl.pallas_call(
         gram_kernel,
@@ -459,9 +465,9 @@
             pl.BlockSpec((pair, channels, row_count, lon_count), lambda g: (g, 0, 0, 0)),
             pl.BlockSpec((row_count, lon_count), lambda g: (0, 0)),
             pl.BlockSpec((row_count, lon_count), lambda g: (0, 0)),
-            pl.BlockSpec((1, lon_count), lambda g: (0, 0)),
-            pl.BlockSpec((pair, channels, lon_count), lambda g: (g, 0, 0)),
-            pl.BlockSpec((pair, channels, lon_count), lambda g: (g, 0, 0)),
+            pl.BlockSpec((8, lon_count), lambda g: (halo // 8, 0)),
+            pl.BlockSpec((pair * channels, lon_count), lambda g: (g, 0)),
+            pl.BlockSpec((pair * channels, lon_count), lambda g: (g, 0)),
             pl.BlockSpec(memory_space=pltpu.VMEM),
             pl.BlockSpec(memory_space=pltpu.SMEM),
             pl.BlockSpec(memory_space=pltpu.SMEM),
@@ -490,7 +496,7 @@
         prior_member_stack,
         zonal_stability_ratio,
         meridional_stability_ratio,
-        south_c,
+        below,
         below,
         above,
         gram,

time: 110 us -> 107 us (0.973)
  starting transfers between devices: 9.01 us -> 3.7 us
  Pallas kernels: 94.7 us -> 97.3 us
    ppermute x1 -> x0, starting transfers between devices: 5.19 us -> none  [fast_device(): south_c = lax.ppermute(edges[2], 'lat', up)]
    pallas_call x1, Pallas kernels: 68.6 us -> 71.1 us  [fast_device(): pl.pallas_call(transport_kernel, grid=(members_dev // pair,), out_shape=(...]
  transfers between devices with their start and end apart: 3 -> 2, of which waited for: 0 -> 0; matrix products, arithmetic and copies ran while one was open for 0% -> 0% of each run, Pallas kernels for 11% -> 11%
where the time goes in v3:
time: 107 us
  Pallas kernels  97.3 us (91%)
  local copies, waits for them, and re-layouts  5.66 us (5%)
  starting transfers between devices  3.7 us (3%)
    pallas_call x1, Pallas kernels, fast_device(): pl.pallas_call(transport_kernel, grid=(members_dev // pair,), out_shape=(...  71.1 us
    pallas_call x1, Pallas kernels, fast_device(): pl.pallas_call(lambda *refs: analysis_kernel(lat_count, row_count, tile_r...  14.5 us
    pallas_call x1, Pallas kernels, fast_device(): pl.pallas_call(gram_kernel, grid=(tiles,), out_shape=jax.ShapeDtypeStruct...  11.7 us
    slice x1, local copies, waits for them, and re-layouts, fast_device(): prior_member_stack[:, :, 0, :].reshape(halo, lon_count)  4.6 us
    ppermute x1, starting transfers between devices, fast_device(): below = lax.ppermute(edges[0], 'lat', up)  2.41 us
  transfers between devices with their start and end apart: 2, of which 0 were waited for; matrix products, arithmetic and copies ran while one was open for 0% of the time, Pallas kernels for 11%

profile of v3, /device:TPU:0, one launch (start us, length us, event | category | flops | bytes accessed | tf_op | source)
XLA Modules:
  0.0 106.8 jit_solution(15629679574013618068)
XLA Ops:
  0.0 0.0 copy-start.4
  0.0 0.0 copy-start.5
  0.0 0.0 copy-start.6
  0.0 0.0 copy-start.1
  0.0 0.0 copy-start
  0.0 0.8 slice.10
  0.8 4.6 %fusion = (f32[16,16,1,512]{3,2,1,0:T(1,128)S(1)}, f32[16,16,1,512]{3,2,1,0:T(1,128)S(1)}) fusion(f32[16,16,8,512]{3,2,1,0:T(8,128)} %prior_ref.1), kind=kLoop, calls=%fused_computation.1 | loop fusion | bytes 2097152 | tf_op jit(solution)/shard_map/slice | solution.py:430
  5.6 2.4 %collective-permute-start = (f32[264,512]{1,0:T(8,128)S(1)}, f32[264,512]{1,0:T(8,128)S(1)}, u32[]{:S(2)}, u32[]{:S(2)}) collective-permute-start(f32[264,512]{1,0:T(8,128)S(1)} %pad_maximum_fusion), channel_id=1, source_target_pairs={{0,1},{1,2},{2,3},{3,4},{4,5},{5,6},{6,7},{8,9},{9,10},{10,11},{11... | collective-permute-start | bytes 1622024 | tf_op jit(solution)/shard_map/ppermute | solution.py:433
  8.0 1.3 %collective-permute-start.1 = (f32[256,512]{1,0:T(8,128)S(1)}, f32[256,512]{1,0:T(8,128)S(1)}, u32[]{:S(2)}, u32[]{:S(2)}) collective-permute-start(f32[256,512]{1,0:T(8,128)S(1)} %bitcast.6), channel_id=1, source_target_pairs={{1,0},{2,1},{3,2},{4,3},{5,4},{6,5},{7,6},{9,8},{10,9},{11,10},{12... | collective-permute-start | bytes 1572872 | tf_op jit(solution)/shard_map/ppermute | solution.py:434
  9.3 0.0 copy-done.5
  9.3 0.1 copy.14.neighbours_ref
  9.4 0.0 copy-done.6
  9.4 0.1 copy.15.localization_ref
  9.5 0.0 copy-done.4
  9.5 0.0 copy-done.1
  9.5 0.0 copy-done
  9.5 0.0 copy-start.2
  9.5 0.0 copy-start.3
  9.5 11.7 %gram.1.gram_ref = f32[16,72,64]{2,1,0:T(8,128)S(1)} custom-call(bf16[16,64,4096]{2,1,0:T(8,128)(2,1)} %perturb_ref.1, f32[16,4096]{1,0:T(8,128)S(1)} %copy-done, f32[16,4096]{1,0:T(8,128)S(1)} %copy-done.1, s32[16]{0:T(128)S(1)} %copy-done.4), custom_call_target="tpu_custom_call" | custom-call | flops 1073741824 | bytes 16777216 | tf_op jit(solution)/shard_map/gram/pallas_call | solution.py:436
  21.2 0.0 collective-permute-done.1.above_ref
  21.2 0.0 collective-permute-done.south_c_ref.below_ref
  21.2 0.0 copy-done.2
  21.2 0.0 copy-done.3
  21.3 71.1 %transport.1 = (bf16[32,128,256]{2,1,0:T(8,128)(2,1)S(1)}, f32[16,64,64]{2,1,0:T(8,128)S(1)}) custom-call(f32[16,16,8,512]{3,2,1,0:T(8,128)} %prior_ref.1, f32[8,512]{1,0:T(8,128)S(1)} %copy-done.3, f32[8,512]{1,0:T(8,128)S(1)} %copy-done.2, f32[264,512]{1,0:T(8,128)S(1)} %collective-permute-done.south_c_ref.below_ref, ...), custom_call_target="tpu_custom_call" | custom-call | tf_op jit(solution)/shard_map/transport/pallas_call | solution.py:457
  92.3 14.5 %analysis.1 = f32[64,16,16,64]{3,2,1,0:T(8,128)} custom-call(f32[16,64,64]{2,1,0:T(8,128)S(1)} %get-tuple-element.13.refs_0_, bf16[4,8,128,256]{3,2,1,0:T(8,128)(2,1)S(1)} %bitcast.4), custom_call_target="tpu_custom_call" | custom-call | tf_op jit(solution)/shard_map/analysis/pallas_call | solution.py:511
  (4 shorter events, 0.1 us)
Async XLA Ops:
  0.0 9.5 %copy-start.4 = (s32[16]{0:T(128)S(1)}, s32[16]{0:T(128)}, u32[]{:S(2)}) copy-start(s32[16]{0:T(128)} %count_ref) | copy-start | bytes 196
  0.0 9.3 %copy-start.5 = (s32[16,6]{0,1:T(8,128)S(1)}, s32[16,6]{0,1:T(8,128)}, u32[]{:S(2)}) copy-start(s32[16,6]{0,1:T(8,128)} %param.16) | copy-start | bytes 1156
  0.0 9.4 %copy-start.6 = (f32[16,6]{0,1:T(8,128)S(1)}, f32[16,6]{0,1:T(8,128)}, u32[]{:S(2)}) copy-start(f32[16,6]{0,1:T(8,128)} %param.17) | copy-start | bytes 1156
  0.0 9.4 %copy-start.1 = (f32[16,4096]{1,0:T(8,128)S(1)}, f32[16,4096]{1,0:T(8,128)}, u32[]{:S(2)}) copy-start(f32[16,4096]{1,0:T(8,128)} %variance_ref.1) | copy-start | bytes 786436
  0.0 9.4 %copy-start = (f32[16,4096]{1,0:T(8,128)S(1)}, f32[16,4096]{1,0:T(8,128)}, u32[]{:S(2)}) copy-start(f32[16,4096]{1,0:T(8,128)} %innovation_ref.1) | copy-start | bytes 786436
  5.6 15.7 %collective-permute-start = (f32[264,512]{1,0:T(8,128)S(1)}, f32[264,512]{1,0:T(8,128)S(1)}, u32[]{:S(2)}, u32[]{:S(2)}) collective-permute-start(f32[264,512]{1,0:T(8,128)S(1)} %pad_maximum_fusion), channel_id=1, source_target_pairs={{0,1},{1,2},{2,3},{3,4},{4,5},{5,6},{6,7},{8,9},{9,10},{10,11},{11... | collective-permute-start | bytes 1622024 | tf_op jit(solution)/shard_map/ppermute | solution.py:433
  8.0 13.2 %collective-permute-start.1 = (f32[256,512]{1,0:T(8,128)S(1)}, f32[256,512]{1,0:T(8,128)S(1)}, u32[]{:S(2)}, u32[]{:S(2)}) collective-permute-start(f32[256,512]{1,0:T(8,128)S(1)} %bitcast.6), channel_id=1, source_target_pairs={{1,0},{2,1},{3,2},{4,3},{5,4},{6,5},{7,6},{9,8},{10,9},{11,10},{12... | collective-permute-start | bytes 1572872 | tf_op jit(solution)/shard_map/ppermute | solution.py:434
  9.5 11.8 %copy-start.2 = (f32[8,512]{1,0:T(8,128)S(1)}, f32[8,512]{1,0:T(8,128)}, u32[]{:S(2)}) copy-start(f32[8,512]{1,0:T(8,128)} %north_ref.1) | copy-start | bytes 49156
  9.5 11.8 %copy-start.3 = (f32[8,512]{1,0:T(8,128)S(1)}, f32[8,512]{1,0:T(8,128)}, u32[]{:S(2)}) copy-start(f32[8,512]{1,0:T(8,128)} %zonal_ref.1) | copy-start | bytes 49156

commit v4 on v3

--- a/solution.py
+++ b/solution.py
@@ -214,11 +214,7 @@
 
     @pl.when(step < bands)
     def _():
-        pick_row = lax.broadcasted_iota(jnp.int32, (wide, per_band * members), 0)
-        pick_col = lax.broadcasted_iota(jnp.int32, (wide, per_band * members), 1)
-        row_bits, tile_bits = rows.bit_length() - 1, tile_rows.bit_length() - 1
-        source = (((pick_row & (rows - 1)) >> tile_bits) * members) + (pick_row >> row_bits)
-        pick = jnp.where(pick_col == source, 1.0, 0.0).astype(jnp.bfloat16)
+        row_bits = rows.bit_length() - 1
         spread_row = lax.broadcasted_iota(jnp.int32, (members, wide), 0)
         spread_col = lax.broadcasted_iota(jnp.int32, (members, wide), 1)
         spread = jnp.where((spread_col >> row_bits) == spread_row, 1.0, 0.0).astype(jnp.bfloat16)
@@ -228,9 +224,14 @@
         mine = weights_ref[...].reshape(per_band * members, members)
         fields = arrived_ref[...].reshape(wide, arrived_ref.shape[-1])
         total = None
+        sub = lax.broadcasted_iota(jnp.int32, (1, rows, wide), 1)
         for part in split(mine):
-            tall = dot(pick, part).astype(jnp.bfloat16)
-            full = jnp.where(diagonal, dot(tall, spread).reshape(members, rows, wide), 0.0)
+            tall = dot(part, spread)
+            full = None
+            for t in range(per_band):
+                piece = tall[t * members : (t + 1) * members].reshape(members, 1, wide)
+                own = diagonal & (sub >= t * tile_rows) & (sub < (t + 1) * tile_rows)
+                full = jnp.where(own, piece, 0.0 if full is None else full)
             full = full.reshape(wide, wide).astype(jnp.bfloat16)
             term = dot(full, fields)
             total = term if total is None else total + term
@@ -255,6 +256,14 @@
         return lax.dot_general(
             a, b, (dims, ((), ())),
             precision=lax.Precision.HIGHEST, preferred_element_type=jnp.float32,
+        )
+
+    def product(a, b):
+        a_hi, a_lo = split(a)
+        b_hi, b_lo = split(b)
+        return dot(
+            jnp.concatenate([a_hi, a_hi, a_lo], axis=1),
+            jnp.concatenate([b_hi, b_lo, b_hi], axis=0),
         )
 
     scales, drives = [], []
@@ -273,9 +282,9 @@
     def one(_, carry):
         for t in range(tiles):
             now, inv = current[t], inverse[t]
-            middle = 1.5 * identity - 0.5 * exact(inv, now)
-            current[t] = exact(now, middle)
-            inverse[t] = exact(middle, inv)
+            middle = 1.5 * identity - 0.5 * product(inv, now)
+            current[t] = product(now, middle)
+            inverse[t] = product(middle, inv)
         return carry
 
     lax.fori_loop(0, NS_ITERS, one, 0)

time: 107 us -> 104 us (0.972)
  Pallas kernels: 97.3 us -> 94.3 us
    pallas_call x1, Pallas kernels: 14.5 us -> 11.5 us  [fast_device(): pl.pallas_call(lambda *refs: analysis_kernel(lat_count, row_count, tile_r...]
where the time goes in v4:
time: 104 us
  Pallas kernels  94.3 us (91%)
  local copies, waits for them, and re-layouts  5.66 us (5%)
  starting transfers between devices  3.7 us (4%)
    pallas_call x1, Pallas kernels, fast_device(): pl.pallas_call(transport_kernel, grid=(members_dev // pair,), out_shape=(...  71.1 us
    pallas_call x1, Pallas kernels, fast_device(): pl.pallas_call(gram_kernel, grid=(tiles,), out_shape=jax.ShapeDtypeStruct...  11.7 us
    pallas_call x1, Pallas kernels, fast_device(): pl.pallas_call(lambda *refs: analysis_kernel(lat_count, row_count, tile_r...  11.5 us
    slice x1, local copies, waits for them, and re-layouts, fast_device(): prior_member_stack[:, :, 0, :].reshape(halo, lon_count)  4.6 us
    ppermute x1, starting transfers between devices, fast_device(): below = lax.ppermute(edges[0], 'lat', up)  2.41 us
  transfers between devices with their start and end apart: 2, of which 0 were waited for; matrix products, arithmetic and copies ran while one was open for 0% of the time, Pallas kernels for 11%

profile of v4, /device:TPU:0, one launch (start us, length us, event | category | flops | bytes accessed | tf_op | source)
XLA Modules:
  0.0 103.8 jit_solution(16236260830321114477)
XLA Ops:
  0.0 0.0 copy-start.4
  0.0 0.0 copy-start.5
  0.0 0.0 copy-start.6
  0.0 0.0 copy-start.1
  0.0 0.0 copy-start
  0.0 0.8 slice.10
  0.8 4.6 %fusion = (f32[16,16,1,512]{3,2,1,0:T(1,128)S(1)}, f32[16,16,1,512]{3,2,1,0:T(1,128)S(1)}) fusion(f32[16,16,8,512]{3,2,1,0:T(8,128)} %prior_ref.1), kind=kLoop, calls=%fused_computation.1 | loop fusion | bytes 2097152 | tf_op jit(solution)/shard_map/slice | solution.py:439
  5.6 2.4 %collective-permute-start = (f32[264,512]{1,0:T(8,128)S(1)}, f32[264,512]{1,0:T(8,128)S(1)}, u32[]{:S(2)}, u32[]{:S(2)}) collective-permute-start(f32[264,512]{1,0:T(8,128)S(1)} %pad_maximum_fusion), channel_id=1, source_target_pairs={{0,1},{1,2},{2,3},{3,4},{4,5},{5,6},{6,7},{8,9},{9,10},{10,11},{11... | collective-permute-start | bytes 1622024 | tf_op jit(solution)/shard_map/ppermute | solution.py:442
  8.0 1.3 %collective-permute-start.1 = (f32[256,512]{1,0:T(8,128)S(1)}, f32[256,512]{1,0:T(8,128)S(1)}, u32[]{:S(2)}, u32[]{:S(2)}) collective-permute-start(f32[256,512]{1,0:T(8,128)S(1)} %bitcast.6), channel_id=1, source_target_pairs={{1,0},{2,1},{3,2},{4,3},{5,4},{6,5},{7,6},{9,8},{10,9},{11,10},{12... | collective-permute-start | bytes 1572872 | tf_op jit(solution)/shard_map/ppermute | solution.py:443
  9.3 0.0 copy-done.5
  9.3 0.1 copy.14.neighbours_ref
  9.4 0.0 copy-done.6
  9.4 0.1 copy.15.localization_ref
  9.5 0.0 copy-done.4
  9.5 0.0 copy-done.1
  9.5 0.0 copy-done
  9.5 0.0 copy-start.2
  9.5 0.0 copy-start.3
  9.5 11.7 %gram.1.gram_ref = f32[16,72,64]{2,1,0:T(8,128)S(1)} custom-call(bf16[16,64,4096]{2,1,0:T(8,128)(2,1)} %perturb_ref.1, f32[16,4096]{1,0:T(8,128)S(1)} %copy-done, f32[16,4096]{1,0:T(8,128)S(1)} %copy-done.1, s32[16]{0:T(128)S(1)} %copy-done.4), custom_call_target="tpu_custom_call" | custom-call | flops 1073741824 | bytes 16777216 | tf_op jit(solution)/shard_map/gram/pallas_call | solution.py:445
  21.2 0.0 collective-permute-done.1.above_ref
  21.2 0.0 collective-permute-done.south_c_ref.below_ref
  21.2 0.0 copy-done.2
  21.2 0.0 copy-done.3
  21.3 71.1 %transport.1 = (bf16[32,128,256]{2,1,0:T(8,128)(2,1)S(1)}, f32[16,64,64]{2,1,0:T(8,128)S(1)}) custom-call(f32[16,16,8,512]{3,2,1,0:T(8,128)} %prior_ref.1, f32[8,512]{1,0:T(8,128)S(1)} %copy-done.3, f32[8,512]{1,0:T(8,128)S(1)} %copy-done.2, f32[264,512]{1,0:T(8,128)S(1)} %collective-permute-done.south_c_ref.below_ref, ...), custom_call_target="tpu_custom_call" | custom-call | tf_op jit(solution)/shard_map/transport/pallas_call | solution.py:466
  92.3 11.5 %analysis.1 = f32[64,16,16,64]{3,2,1,0:T(8,128)} custom-call(f32[16,64,64]{2,1,0:T(8,128)S(1)} %get-tuple-element.13.refs_0_, bf16[4,8,128,256]{3,2,1,0:T(8,128)(2,1)S(1)} %bitcast.4), custom_call_target="tpu_custom_call" | custom-call | tf_op jit(solution)/shard_map/analysis/pallas_call | solution.py:520
  (4 shorter events, 0.1 us)
Async XLA Ops:
  0.0 9.5 %copy-start.4 = (s32[16]{0:T(128)S(1)}, s32[16]{0:T(128)}, u32[]{:S(2)}) copy-start(s32[16]{0:T(128)} %count_ref) | copy-start | bytes 196
  0.0 9.3 %copy-start.5 = (s32[16,6]{0,1:T(8,128)S(1)}, s32[16,6]{0,1:T(8,128)}, u32[]{:S(2)}) copy-start(s32[16,6]{0,1:T(8,128)} %param.16) | copy-start | bytes 1156
  0.0 9.4 %copy-start.6 = (f32[16,6]{0,1:T(8,128)S(1)}, f32[16,6]{0,1:T(8,128)}, u32[]{:S(2)}) copy-start(f32[16,6]{0,1:T(8,128)} %param.17) | copy-start | bytes 1156
  0.0 9.4 %copy-start.1 = (f32[16,4096]{1,0:T(8,128)S(1)}, f32[16,4096]{1,0:T(8,128)}, u32[]{:S(2)}) copy-start(f32[16,4096]{1,0:T(8,128)} %variance_ref.1) | copy-start | bytes 786436
  0.0 9.4 %copy-start = (f32[16,4096]{1,0:T(8,128)S(1)}, f32[16,4096]{1,0:T(8,128)}, u32[]{:S(2)}) copy-start(f32[16,4096]{1,0:T(8,128)} %innovation_ref.1) | copy-start | bytes 786436
  5.6 15.7 %collective-permute-start = (f32[264,512]{1,0:T(8,128)S(1)}, f32[264,512]{1,0:T(8,128)S(1)}, u32[]{:S(2)}, u32[]{:S(2)}) collective-permute-start(f32[264,512]{1,0:T(8,128)S(1)} %pad_maximum_fusion), channel_id=1, source_target_pairs={{0,1},{1,2},{2,3},{3,4},{4,5},{5,6},{6,7},{8,9},{9,10},{10,11},{11... | collective-permute-start | bytes 1622024 | tf_op jit(solution)/shard_map/ppermute | solution.py:442
  8.0 13.2 %collective-permute-start.1 = (f32[256,512]{1,0:T(8,128)S(1)}, f32[256,512]{1,0:T(8,128)S(1)}, u32[]{:S(2)}, u32[]{:S(2)}) collective-permute-start(f32[256,512]{1,0:T(8,128)S(1)} %bitcast.6), channel_id=1, source_target_pairs={{1,0},{2,1},{3,2},{4,3},{5,4},{6,5},{7,6},{9,8},{10,9},{11,10},{12... | collective-permute-start | bytes 1572872 | tf_op jit(solution)/shard_map/ppermute | solution.py:443
  9.5 11.8 %copy-start.2 = (f32[8,512]{1,0:T(8,128)S(1)}, f32[8,512]{1,0:T(8,128)}, u32[]{:S(2)}) copy-start(f32[8,512]{1,0:T(8,128)} %north_ref.1) | copy-start | bytes 49156
  9.5 11.8 %copy-start.3 = (f32[8,512]{1,0:T(8,128)S(1)}, f32[8,512]{1,0:T(8,128)}, u32[]{:S(2)}) copy-start(f32[8,512]{1,0:T(8,128)} %zonal_ref.1) | copy-start | bytes 49156

commit v5 on v4

--- a/solution.py
+++ b/solution.py
@@ -460,7 +460,7 @@
         name="gram",
     )(obs_perturb, innovation, inverse_error_variance, obs_count)
 
-    pair, chunks = 2, 4
+    pair, chunks = 2, 8
     wire = (devices, members_dev * row_count, channels * strip)
     square = (tiles, members, members)
     arrived, folded = pl.pallas_call(

time: 104 us -> 107 us (1.029)
  Pallas kernels: 94.3 us -> 97 us
    pallas_call x1, Pallas kernels: 71.1 us -> 73.8 us  [fast_device(): pl.pallas_call(transport_kernel, grid=(members_dev // pair,), out_shape=(...]
where the time goes in v5:
time: 107 us
  Pallas kernels  97 us (91%)
  local copies, waits for them, and re-layouts  5.66 us (5%)
  starting transfers between devices  3.7 us (3%)
    pallas_call x1, Pallas kernels, fast_device(): pl.pallas_call(transport_kernel, grid=(members_dev // pair,), out_shape=(...  73.8 us
    pallas_call x1, Pallas kernels, fast_device(): pl.pallas_call(gram_kernel, grid=(tiles,), out_shape=jax.ShapeDtypeStruct...  11.7 us
    pallas_call x1, Pallas kernels, fast_device(): pl.pallas_call(lambda *refs: analysis_kernel(lat_count, row_count, tile_r...  11.5 us
    slice x1, local copies, waits for them, and re-layouts, fast_device(): prior_member_stack[:, :, 0, :].reshape(halo, lon_count)  4.6 us
    ppermute x1, starting transfers between devices, fast_device(): below = lax.ppermute(edges[0], 'lat', up)  2.41 us
  transfers between devices with their start and end apart: 2, of which 0 were waited for; matrix products, arithmetic and copies ran while one was open for 0% of the time, Pallas kernels for 11%

profile of v5, /device:TPU:0, one launch (start us, length us, event | category | flops | bytes accessed | tf_op | source)
XLA Modules:
  0.0 106.5 jit_solution(14219634076503388853)
XLA Ops:
  0.0 0.0 copy-start.4
  0.0 0.0 copy-start.5
  0.0 0.0 copy-start.6
  0.0 0.0 copy-start.1
  0.0 0.0 copy-start
  0.0 0.8 slice.10
  0.8 4.6 %fusion = (f32[16,16,1,512]{3,2,1,0:T(1,128)S(1)}, f32[16,16,1,512]{3,2,1,0:T(1,128)S(1)}) fusion(f32[16,16,8,512]{3,2,1,0:T(8,128)} %prior_ref.1), kind=kLoop, calls=%fused_computation.1 | loop fusion | bytes 2097152 | tf_op jit(solution)/shard_map/slice | solution.py:439
  5.6 2.4 %collective-permute-start = (f32[264,512]{1,0:T(8,128)S(1)}, f32[264,512]{1,0:T(8,128)S(1)}, u32[]{:S(2)}, u32[]{:S(2)}) collective-permute-start(f32[264,512]{1,0:T(8,128)S(1)} %pad_maximum_fusion), channel_id=1, source_target_pairs={{0,1},{1,2},{2,3},{3,4},{4,5},{5,6},{6,7},{8,9},{9,10},{10,11},{11... | collective-permute-start | bytes 1622024 | tf_op jit(solution)/shard_map/ppermute | solution.py:442
  8.0 1.3 %collective-permute-start.1 = (f32[256,512]{1,0:T(8,128)S(1)}, f32[256,512]{1,0:T(8,128)S(1)}, u32[]{:S(2)}, u32[]{:S(2)}) collective-permute-start(f32[256,512]{1,0:T(8,128)S(1)} %bitcast.6), channel_id=1, source_target_pairs={{1,0},{2,1},{3,2},{4,3},{5,4},{6,5},{7,6},{9,8},{10,9},{11,10},{12... | collective-permute-start | bytes 1572872 | tf_op jit(solution)/shard_map/ppermute | solution.py:443
  9.3 0.0 copy-done.5
  9.3 0.1 copy.14.neighbours_ref
  9.4 0.0 copy-done.6
  9.4 0.1 copy.15.localization_ref
  9.5 0.0 copy-done.4
  9.5 0.0 copy-done.1
  9.5 0.0 copy-done
  9.5 0.0 copy-start.2
  9.5 0.0 copy-start.3
  9.5 11.7 %gram.1.gram_ref = f32[16,72,64]{2,1,0:T(8,128)S(1)} custom-call(bf16[16,64,4096]{2,1,0:T(8,128)(2,1)} %perturb_ref.1, f32[16,4096]{1,0:T(8,128)S(1)} %copy-done, f32[16,4096]{1,0:T(8,128)S(1)} %copy-done.1, s32[16]{0:T(128)S(1)} %copy-done.4), custom_call_target="tpu_custom_call" | custom-call | flops 1073741824 | bytes 16777216 | tf_op jit(solution)/shard_map/gram/pallas_call | solution.py:445
  21.2 0.0 collective-permute-done.1.above_ref
  21.2 0.0 collective-permute-done.south_c_ref.below_ref
  21.2 0.0 copy-done.2
  21.2 0.0 copy-done.3
  21.3 73.8 %transport.1 = (bf16[32,128,256]{2,1,0:T(8,128)(2,1)S(1)}, f32[16,64,64]{2,1,0:T(8,128)S(1)}) custom-call(f32[16,16,8,512]{3,2,1,0:T(8,128)} %prior_ref.1, f32[8,512]{1,0:T(8,128)S(1)} %copy-done.3, f32[8,512]{1,0:T(8,128)S(1)} %copy-done.2, f32[264,512]{1,0:T(8,128)S(1)} %collective-permute-done.south_c_ref.below_ref, ...), custom_call_target="tpu_custom_call" | custom-call | tf_op jit(solution)/shard_map/transport/pallas_call | solution.py:466
  95.0 11.5 %analysis.1 = f32[64,16,16,64]{3,2,1,0:T(8,128)} custom-call(f32[16,64,64]{2,1,0:T(8,128)S(1)} %get-tuple-element.13.refs_0_, bf16[4,8,128,256]{3,2,1,0:T(8,128)(2,1)S(1)} %bitcast.4), custom_call_target="tpu_custom_call" | custom-call | tf_op jit(solution)/shard_map/analysis/pallas_call | solution.py:520
  (4 shorter events, 0.1 us)
Async XLA Ops:
  0.0 9.5 %copy-start.4 = (s32[16]{0:T(128)S(1)}, s32[16]{0:T(128)}, u32[]{:S(2)}) copy-start(s32[16]{0:T(128)} %count_ref) | copy-start | bytes 196
  0.0 9.3 %copy-start.5 = (s32[16,6]{0,1:T(8,128)S(1)}, s32[16,6]{0,1:T(8,128)}, u32[]{:S(2)}) copy-start(s32[16,6]{0,1:T(8,128)} %param.16) | copy-start | bytes 1156
  0.0 9.4 %copy-start.6 = (f32[16,6]{0,1:T(8,128)S(1)}, f32[16,6]{0,1:T(8,128)}, u32[]{:S(2)}) copy-start(f32[16,6]{0,1:T(8,128)} %param.17) | copy-start | bytes 1156
  0.0 9.4 %copy-start.1 = (f32[16,4096]{1,0:T(8,128)S(1)}, f32[16,4096]{1,0:T(8,128)}, u32[]{:S(2)}) copy-start(f32[16,4096]{1,0:T(8,128)} %variance_ref.1) | copy-start | bytes 786436
  0.0 9.4 %copy-start = (f32[16,4096]{1,0:T(8,128)S(1)}, f32[16,4096]{1,0:T(8,128)}, u32[]{:S(2)}) copy-start(f32[16,4096]{1,0:T(8,128)} %innovation_ref.1) | copy-start | bytes 786436
  5.6 15.7 %collective-permute-start = (f32[264,512]{1,0:T(8,128)S(1)}, f32[264,512]{1,0:T(8,128)S(1)}, u32[]{:S(2)}, u32[]{:S(2)}) collective-permute-start(f32[264,512]{1,0:T(8,128)S(1)} %pad_maximum_fusion), channel_id=1, source_target_pairs={{0,1},{1,2},{2,3},{3,4},{4,5},{5,6},{6,7},{8,9},{9,10},{10,11},{11... | collective-permute-start | bytes 1622024 | tf_op jit(solution)/shard_map/ppermute | solution.py:442
  8.0 13.2 %collective-permute-start.1 = (f32[256,512]{1,0:T(8,128)S(1)}, f32[256,512]{1,0:T(8,128)S(1)}, u32[]{:S(2)}, u32[]{:S(2)}) collective-permute-start(f32[256,512]{1,0:T(8,128)S(1)} %bitcast.6), channel_id=1, source_target_pairs={{1,0},{2,1},{3,2},{4,3},{5,4},{6,5},{7,6},{9,8},{10,9},{11,10},{12... | collective-permute-start | bytes 1572872 | tf_op jit(solution)/shard_map/ppermute | solution.py:443
  9.5 11.8 %copy-start.2 = (f32[8,512]{1,0:T(8,128)S(1)}, f32[8,512]{1,0:T(8,128)}, u32[]{:S(2)}) copy-start(f32[8,512]{1,0:T(8,128)} %north_ref.1) | copy-start | bytes 49156
  9.5 11.8 %copy-start.3 = (f32[8,512]{1,0:T(8,128)S(1)}, f32[8,512]{1,0:T(8,128)}, u32[]{:S(2)}) copy-start(f32[8,512]{1,0:T(8,128)} %zonal_ref.1) | copy-start | bytes 49156
